TPU v7x, 256 devices: a whole 4x4x8 slice. The times are simulated.
256 devices in a mesh: sec: 4 (over x), tile: 64 (over z, y, core).
Axes of the slice: x: 4, y: 4, z: 8, core: 2. Of those that a mesh axis runs over, the one named last changes fastest.
Arguments:
- sections: bfloat16 [8, 64, 256, 512], P('sec', 'tile'), may hold values from -40 to 40
- corner_offsets: int32 [2, 8, 64, 256, 512], P(None, 'sec', 'tile'), may hold values from -2 to 1
Outputs:
- node_mesh: float32 [8, 2, 64, 8, 16], P('sec', None, 'tile')
- warped: float32 [8, 64, 256, 512], P('sec', 'tile')
All inputs are finite; a program needn't handle non-finite values.
Results may differ from a plain program's by a relative error of at most 0.0035.
Values may be sent and summed in bfloat16 or wider, within the bound.
A program may use at most 64 MiB of HBM per device.

v0:
```python
import math

import jax
import jax.numpy as jnp
from jax import lax
from jax.sharding import PartitionSpec as P

TILE_GRID = 8
PATCH = 128
STRIDE = 32
SHIFTS = 32
ITERS = 4
HALO = 48


EPS = 1e-05
STEP_RATE = 0.15


def from_behind(value, axis, steps):
    count = lax.axis_size(axis)
    initial, last = (max(0, -steps), min(count, count - steps))
    return lax.ppermute(value, axis, [(source, source + steps) for source in range(initial, last)])


def padded_2(block, sides, width):
    for axis, dim in sides:
        count = lax.axis_size(axis)
        forward = [(i, i + 1) for i in range(count - 1)]
        backward = [(target, source) for source, target in forward]
        low = lax.ppermute(
            lax.slice_in_dim(block, block.shape[dim] - width, None, axis=dim), axis, forward
        )
        high = lax.ppermute(lax.slice_in_dim(block, 0, width, axis=dim), axis, backward)
        block = jnp.concatenate([low, block, high], axis=dim)
    return block


def dft_tables(patch_size, shift_count):
    counter = jnp.arange(patch_size, dtype=jnp.int32)
    forward = counter[:, None] * counter[None, :] % patch_size
    angles = forward.astype(jnp.float32) * (2.0 * math.pi / patch_size)
    shift_values = jnp.arange(shift_count, dtype=jnp.int32) - shift_count // 2
    backward = shift_values[:, None] * counter[None, :] % patch_size
    back_angles = backward.astype(jnp.float32) * (2.0 * math.pi / patch_size)
    return (
        jnp.cos(angles).astype(jnp.bfloat16),
        jnp.sin(angles).astype(jnp.bfloat16),
        jnp.cos(back_angles).astype(jnp.bfloat16),
        jnp.sin(back_angles).astype(jnp.bfloat16),
    )


def window_patches(row_band, stride):
    stack_count, patch_size, band_width = row_band.shape
    patch_count = (band_width - patch_size) // stride + 1
    blocks = row_band.reshape(stack_count, patch_size, band_width // stride, stride)
    pieces = [
        blocks[:, :, offset : offset + patch_count, :] for offset in range(patch_size // stride)
    ]
    joined = jnp.stack(pieces, 3).reshape(stack_count, patch_size, patch_count, patch_size)
    return jnp.transpose(joined, (0, 2, 1, 3))


def spectral_product(form, left, right):
    return jnp.einsum(form, left, right, preferred_element_type=jnp.float32)


def spectrum(patches, tables):
    cosine_lookup, sine_lookup = (tables[0], tables[1])
    real_row_pass = spectral_product("jpq,qk->jpk", patches, cosine_lookup).astype(jnp.bfloat16)
    imaginary_row_pass = (-spectral_product("jpq,qk->jpk", patches, sine_lookup)).astype(
        jnp.bfloat16
    )
    real_complete = (
        spectral_product("gh,tho->tgo", cosine_lookup, real_row_pass)
        + spectral_product("gh,tho->tgo", sine_lookup, imaginary_row_pass)
    ).astype(jnp.bfloat16)
    imaginary_complete = (
        spectral_product("gh,tho->tgo", cosine_lookup, imaginary_row_pass)
        - spectral_product("gh,tho->tgo", sine_lookup, real_row_pass)
    ).astype(jnp.bfloat16)
    return (real_complete, imaginary_complete)


def patch_energy(patches):
    values = patches.astype(jnp.float32)
    return jnp.mean(values * values, axis=(1, 2)) + EPS


def displacement(current, current_energy, later, later_energy, tables):
    back_cos, back_sin = (tables[2], tables[3])
    shift_count, patch_size = back_cos.shape
    first_real = current[0].astype(jnp.float32)
    first_imag = current[1].astype(jnp.float32)
    second_real = later[0].astype(jnp.float32)
    second_imag = later[1].astype(jnp.float32)
    cross_real = (first_real * second_real + first_imag * second_imag).astype(jnp.bfloat16)
    cross_imag = (first_real * second_imag - first_imag * second_real).astype(jnp.bfloat16)
    half_real = (
        spectral_product("uk,jkm->jum", back_cos, cross_real)
        - spectral_product("uk,jkm->jum", back_sin, cross_imag)
    ).astype(jnp.bfloat16)
    half_imag = (
        spectral_product("uk,jkm->jum", back_cos, cross_imag)
        + spectral_product("uk,jkm->jum", back_sin, cross_real)
    ).astype(jnp.bfloat16)
    correlation = (
        spectral_product("jum,vm->juv", half_real, back_cos)
        - spectral_product("jum,vm->juv", half_imag, back_sin)
    ) / float(patch_size * patch_size)
    scale_term = patch_size * patch_size * jnp.sqrt(current_energy * later_energy)
    weights = jnp.exp(patch_size / 2.0 * correlation / scale_term[:, None, None])
    total = jnp.sum(weights, axis=(1, 2))
    shift_values = (jnp.arange(shift_count, dtype=jnp.int32) - shift_count // 2).astype(jnp.float32)
    along_rows = jnp.sum(weights * shift_values[None, :, None], axis=(1, 2)) / total
    along_cols = jnp.sum(weights * shift_values[None, None, :], axis=(1, 2)) / total
    return jnp.stack([along_rows, along_cols], 0)


def section_flows(padded, tables, node_rows):
    own_count = padded.shape[0] - 1

    def node_row(row_number):
        row_band = lax.dynamic_slice_in_dim(padded, row_number * STRIDE, PATCH, 1)
        patches = window_patches(row_band, STRIDE)
        later = spectrum(patches[own_count], tables)
        later_energy = patch_energy(patches[own_count])
        collected = []
        for section in range(own_count - 1, -1, -1):
            current = spectrum(patches[section], tables)
            current_energy = patch_energy(patches[section])
            collected.append(displacement(current, current_energy, later, later_energy, tables))
            later, later_energy = (current, current_energy)
        return jnp.stack(collected[::-1], 0)

    flows = lax.map(node_row, jnp.arange(node_rows, dtype=jnp.int32))
    return jnp.transpose(flows, (1, 2, 0, 3))


def pixel_cols_from(piece, shift_by):
    return from_behind(piece, "tile", shift_by)


def pixel_rows_from(piece, shift_by):
    return from_behind(piece, "tile", shift_by)


def frame_tiles(pixels, col_pos):
    from_left = pixel_cols_from(pixels[:, :, -HALO:], 1)
    from_right = pixel_cols_from(pixels[:, :, :HALO], -1)
    from_left = jnp.where(col_pos > 0, from_left, jnp.zeros_like(from_left))
    from_right = jnp.where(col_pos < TILE_GRID - 1, from_right, jnp.zeros_like(from_right))
    widened = jnp.concatenate([from_left, pixels, from_right], 2)
    from_above = pixel_rows_from(widened[:, -HALO:], TILE_GRID)
    from_below = pixel_rows_from(widened[:, :HALO], -TILE_GRID)
    return jnp.concatenate([from_above, widened, from_below], 1)


def node_cols_from(piece, shift_by):
    return from_behind(piece, "tile", shift_by)


def node_rows_from(piece, shift_by):
    return from_behind(piece, "tile", shift_by)


def node_around(field, col_pos):
    from_left = node_cols_from(field[..., -1:], 1)
    from_right = node_cols_from(field[..., :1], -1)
    from_left = jnp.where(col_pos > 0, from_left, jnp.zeros_like(from_left))
    from_right = jnp.where(col_pos < TILE_GRID - 1, from_right, jnp.zeros_like(from_right))
    from_above = node_rows_from(field[:, :, -1:, :], TILE_GRID)
    from_below = node_rows_from(field[:, :, :1, :], -TILE_GRID)
    rows_framed = jnp.concatenate([from_above, field, from_below], 2)
    cols_framed = jnp.concatenate([from_left, field, from_right], 3)
    return (
        rows_framed[:, :, 2:]
        + rows_framed[:, :, :-2]
        + cols_framed[..., 2:]
        + cols_framed[..., :-2]
    )


def warp_sections(padded_own, corner_offsets, node_mesh):
    own_count, padded_rows, padded_cols = padded_own.shape
    pixel_rows = padded_rows - 2 * HALO
    pixel_cols = padded_cols - 2 * HALO
    shift_rows = jnp.repeat(jnp.repeat(node_mesh[:, 0], STRIDE, 1), STRIDE, 2)
    shift_cols = jnp.repeat(jnp.repeat(node_mesh[:, 1], STRIDE, 1), STRIDE, 2)
    row_offset = corner_offsets[0]
    col_offset = corner_offsets[1]
    row_frac = shift_rows - row_offset.astype(jnp.float32)
    col_frac = shift_cols - col_offset.astype(jnp.float32)
    result = jnp.zeros((own_count, pixel_rows, pixel_cols), jnp.float32)
    for row_step in range(-2, 3):
        row_weight = jnp.where(row_offset == row_step, 1.0 - row_frac, 0.0) + jnp.where(
            row_offset + 1 == row_step, row_frac, 0.0
        )
        inner = jnp.zeros((own_count, pixel_rows, pixel_cols), jnp.float32)
        for col_step in range(-2, 3):
            col_weight = jnp.where(col_offset == col_step, 1.0 - col_frac, 0.0) + jnp.where(
                col_offset + 1 == col_step, col_frac, 0.0
            )
            view = padded_own[
                :,
                HALO + row_step : HALO + row_step + pixel_rows,
                HALO + col_step : HALO + col_step + pixel_cols,
            ].astype(jnp.float32)
            inner = inner + col_weight * view
        result = result + row_weight * inner
    return result


def shards(sections, corner_offsets):
    own_count = sections.shape[0]
    pixels = sections[:, 0]
    offsets = corner_offsets[:, :, 0]
    node_rows = pixels.shape[1] // STRIDE
    tile_number = lax.axis_index("tile")
    col_pos = tile_number % TILE_GRID
    sec_total = own_count * lax.axis_size("sec")
    sec_start = lax.axis_index("sec") * own_count
    tables = dft_tables(PATCH, SHIFTS)
    following = from_behind(pixels[:1], "sec", -1)
    padded = frame_tiles(jnp.concatenate([pixels, following], 0), col_pos)
    sec_place = sec_start + jnp.arange(own_count, dtype=jnp.int32)
    has_next = (sec_place < sec_total - 1).astype(jnp.float32)
    flow = section_flows(padded, tables, node_rows) * has_next[:, None, None, None]
    before = from_behind(flow[-1:], "sec", 1)
    flow_prev = jnp.concatenate([before, flow[:-1]], 0)
    not_first = (sec_place > 0).astype(jnp.float32)[:, None, None, None]
    node_mesh = jnp.zeros_like(flow)
    for step_number in range(ITERS):
        sec_framed = padded_2(node_mesh, (("sec", 0),), 1)
        spring = node_mesh - sec_framed[2:] - flow
        earlier = (sec_framed[:own_count] - node_mesh - flow_prev) * not_first
        beside_all = node_around(node_mesh, col_pos)
        node_mesh = node_mesh - STEP_RATE * (spring - earlier + 4.0 * node_mesh - beside_all)
    warped = warp_sections(padded[:own_count], offsets, node_mesh)
    return (node_mesh[:, :, None], warped[:, None])


def solution(mesh):
    in_specs = (P("sec", "tile", None, None), P(None, "sec", "tile", None, None))
    out_specs = (P("sec", None, "tile", None, None), P("sec", "tile", None, None))
    return jax.shard_map(shards, mesh=mesh, in_specs=in_specs, out_specs=out_specs, check_vma=False)
```

profile of v0, /device:TPU:98, one launch (start us, length us, event | category | flops | bytes accessed | tf_op | source)
XLA Modules:
  0.0 316.0 jit_solution(9893291817181451904)
XLA Ops:
  1.2 5.0 %collective-permute-start.9 = (f32[2,2,1,16]{3,2,1,0:T(1,128)}, f32[2,2,1,16]{3,2,1,0:T(1,128)}, u32[]{:S(2)}, u32[]{:S(2)}) collective-permute-start(f32[2,2,1,16]{3,2,1,0:T(1,128)} %broadcast.244), channel_id=1, source_target_pairs={{0,8},{1,9},{2,10},{3,11},{4,12},{5,13},{6,14},{7,15},{8,16},{9,17... | collective-permute-start | bytes 776 | tf_op jit(solution)/shard_map/ppermute | solution.py:23
  6.2 1.9 collective-permute-start.8
  10.7 5.8 %collective-permute-start.10 = (f32[2,2,8,1]{3,2,1,0:T(8,128)}, f32[2,2,8,1]{3,2,1,0:T(8,128)}, u32[]{:S(2)}, u32[]{:S(2)}) collective-permute-start(f32[2,2,8,1]{3,2,1,0:T(8,128)} %broadcast.245), channel_id=1, source_target_pairs={{1,0},{2,1},{3,2},{4,3},{5,4},{6,5},{7,6},{8,7},{9,8},{10,9},{11,1... | collective-permute-start | bytes 392 | tf_op jit(solution)/shard_map/ppermute | solution.py:23
  18.3 2.4 collective-permute-start.1
  27.6 3.4 %collective-permute-start.6 = (f32[1,2,8,16]{3,2,1,0:T(8,128)}, f32[1,2,8,16]{3,2,1,0:T(8,128)}, u32[]{:S(2)}, u32[]{:S(2)}) collective-permute-start(f32[1,2,8,16]{3,2,1,0:T(8,128)} %broadcast.237), channel_id=1, source_target_pairs={{0,64},{64,128},{128,192},{1,65},{65,129},{129,193},{2,66},{66,130... | collective-permute-start | bytes 3080 | tf_op jit(solution)/shard_map/ppermute | solution.py:31
  31.0 1.9 collective-permute-start.2
  33.6 5.2 %collective-permute-done.2 = bf16[3,256,48]{1,2,0:T(8,128)(2,1)S(1)} collective-permute-done((bf16[3,256,48]{1,2,0:T(8,128)(2,1)S(1)}, bf16[3,256,48]{1,2,0:T(8,128)(2,1)S(1)}, u32[]{:S(2)}, u32[]{:S(2)}) %collective-permute-start.2) | collective-permute-done | bytes 73760 | tf_op jit(solution)/shard_map/ppermute | solution.py:23
  40.7 1.9 collective-permute-done.3
  43.0 7.6 %collective-permute-start.4 = (bf16[3,48,608]{1,2,0:T(8,128)(2,1)S(1)}, bf16[3,48,608]{1,2,0:T(8,128)(2,1)S(1)}, u32[]{:S(2)}, u32[]{:S(2)}) collective-permute-start(bf16[3,48,608]{1,2,0:T(8,128)(2,1)S(1)} %get-tuple-element.340), channel_id=1, source_target_pairs={{0,8},{1,9},{2,10},{3,11},{4,12},{5,13},{6,14},{7,15},{8,16},{9,17... | collective-permute-start | bytes 525320 | tf_op jit(solution)/shard_map/ppermute | solution.py:23
  55.1 4.9 %collective-permute-done.4 = bf16[3,48,608]{1,2,0:T(8,128)(2,1)S(1)} collective-permute-done((bf16[3,48,608]{1,2,0:T(8,128)(2,1)S(1)}, bf16[3,48,608]{1,2,0:T(8,128)(2,1)S(1)}, u32[]{:S(2)}, u32[]{:S(2)}) %collective-permute-start.4) | collective-permute-done | bytes 175136 | tf_op jit(solution)/shard_map/ppermute | solution.py:23
  60.1 3.0 collective-permute-start
  63.1 2.3 collective-permute-done.5
  66.3 161.3 %while.16 = (s32[]{:T(128)}, f32[8,2,2,16]{3,0,2,1:T(8,128)}, s32[8]{0:T(128)S(1)}, bf16[3,352,608]{1,2,0:T(8,128)(2,1)S(1)}, s32[32]{0:T(128)}, /*index=5*/s32[]{:T(128)}, s32[1]{0:T(128)}, s32[]{:T(128)}, s32[]{:T(128)}) while((s32[]{:T(128)}, f32[8,2,2,16]{3,0,2,1:T(8,128)}, s32[8]{0:T(128)S(1)}, ...), condition=%wide.region_10.11_spmd.clone.clone.clone, body=%wide.region_0.10_spmd.clone.clone.clone.sunk | while | flops 1380892672 | bytes 64559056 | solution.py:137
  228.4 3.6 %collective-permute-start.7 = (f32[1,2,8,16]{3,2,1,0:T(8,128)S(1)}, f32[1,2,8,16]{3,2,1,0:T(8,128)S(1)}, u32[]{:S(2)}, u32[]{:S(2)}) collective-permute-start(f32[1,2,8,16]{3,2,1,0:T(8,128)S(1)} %get-tuple-element.366), channel_id=1, source_target_pairs={{0,64},{64,128},{128,192},{1,65},{65,129},{129,193},{2,66},{66,130... | collective-permute-start | bytes 3080 | tf_op jit(solution)/shard_map/ppermute | solution.py:23
  232.0 3.1 maximum_maximum_fusion
  238.1 5.1 %collective-permute-start.15 = (f32[2,2,1,16]{3,2,1,0:T(1,128)S(1)}, f32[2,2,1,16]{3,2,1,0:T(1,128)S(1)}, u32[]{:S(2)}, u32[]{:S(2)}) collective-permute-start(f32[2,2,1,16]{3,2,1,0:T(1,128)S(1)} %get-tuple-element.363), channel_id=1, source_target_pairs={{0,8},{1,9},{2,10},{3,11},{4,12},{5,13},{6,14},{7,15},{8,16},{9,17... | collective-permute-start | bytes 776 | tf_op jit(solution)/shard_map/ppermute | solution.py:23
  243.2 2.4 collective-permute-start.12
  247.6 3.4 %collective-permute-start.13 = (f32[1,2,8,16]{3,2,1,0:T(8,128)S(1)}, f32[1,2,8,16]{3,2,1,0:T(8,128)S(1)}, u32[]{:S(2)}, u32[]{:S(2)}) collective-permute-start(f32[1,2,8,16]{3,2,1,0:T(8,128)S(1)} %get-tuple-element.361), channel_id=1, source_target_pairs={{0,64},{64,128},{128,192},{1,65},{65,129},{129,193},{2,66},{66,130... | collective-permute-start | bytes 3080 | tf_op jit(solution)/shard_map/ppermute | solution.py:31
  251.0 2.1 collective-permute-start.17
  253.2 5.0 %collective-permute-done.17 = f32[2,2,8,1]{3,2,1,0:T(8,128)S(1)} collective-permute-done((f32[2,2,8,1]{3,2,1,0:T(8,128)S(1)}, f32[2,2,8,1]{3,2,1,0:T(8,128)S(1)}, u32[]{:S(2)}, u32[]{:S(2)}) %collective-permute-start.17) | collective-permute-done | bytes 160 | tf_op jit(solution)/shard_map/ppermute | solution.py:23
  260.3 5.1 %collective-permute-start.21 = (f32[2,2,1,16]{3,2,1,0:T(1,128)S(1)}, f32[2,2,1,16]{3,2,1,0:T(1,128)S(1)}, u32[]{:S(2)}, u32[]{:S(2)}) collective-permute-start(f32[2,2,1,16]{3,2,1,0:T(1,128)S(1)} %get-tuple-element.357), channel_id=1, source_target_pairs={{0,8},{1,9},{2,10},{3,11},{4,12},{5,13},{6,14},{7,15},{8,16},{9,17... | collective-permute-start | bytes 776 | tf_op jit(solution)/shard_map/ppermute | solution.py:23
  265.5 2.4 collective-permute-start.18
  269.8 3.4 %collective-permute-start.19 = (f32[1,2,8,16]{3,2,1,0:T(8,128)S(1)}, f32[1,2,8,16]{3,2,1,0:T(8,128)S(1)}, u32[]{:S(2)}, u32[]{:S(2)}) collective-permute-start(f32[1,2,8,16]{3,2,1,0:T(8,128)S(1)} %get-tuple-element.355), channel_id=1, source_target_pairs={{0,64},{64,128},{128,192},{1,65},{65,129},{129,193},{2,66},{66,130... | collective-permute-start | bytes 3080 | tf_op jit(solution)/shard_map/ppermute | solution.py:31
  273.3 2.1 collective-permute-start.23
  275.4 5.0 %collective-permute-done.23 = f32[2,2,8,1]{3,2,1,0:T(8,128)S(1)} collective-permute-done((f32[2,2,8,1]{3,2,1,0:T(8,128)S(1)}, f32[2,2,8,1]{3,2,1,0:T(8,128)S(1)}, u32[]{:S(2)}, u32[]{:S(2)}) %collective-permute-start.23) | collective-permute-done | bytes 160 | tf_op jit(solution)/shard_map/ppermute | solution.py:23
  282.6 5.1 %collective-permute-start.27 = (f32[2,2,1,16]{3,2,1,0:T(1,128)S(1)}, f32[2,2,1,16]{3,2,1,0:T(1,128)S(1)}, u32[]{:S(2)}, u32[]{:S(2)}) collective-permute-start(f32[2,2,1,16]{3,2,1,0:T(1,128)S(1)} %get-tuple-element.351), channel_id=1, source_target_pairs={{0,8},{1,9},{2,10},{3,11},{4,12},{5,13},{6,14},{7,15},{8,16},{9,17... | collective-permute-start | bytes 776 | tf_op jit(solution)/shard_map/ppermute | solution.py:23
  287.7 2.4 collective-permute-start.24
  292.1 3.4 %collective-permute-start.25 = (f32[1,2,8,16]{3,2,1,0:T(8,128)S(1)}, f32[1,2,8,16]{3,2,1,0:T(8,128)S(1)}, u32[]{:S(2)}, u32[]{:S(2)}) collective-permute-start(f32[1,2,8,16]{3,2,1,0:T(8,128)S(1)} %get-tuple-element.349), channel_id=1, source_target_pairs={{0,64},{64,128},{128,192},{1,65},{65,129},{129,193},{2,66},{66,130... | collective-permute-start | bytes 3080 | tf_op jit(solution)/shard_map/ppermute | solution.py:31
  295.5 2.1 collective-permute-start.29
  297.7 5.0 %collective-permute-done.29 = f32[2,2,8,1]{3,2,1,0:T(8,128)S(1)} collective-permute-done((f32[2,2,8,1]{3,2,1,0:T(8,128)S(1)}, f32[2,2,8,1]{3,2,1,0:T(8,128)S(1)}, u32[]{:S(2)}, u32[]{:S(2)}) %collective-permute-start.29) | collective-permute-done | bytes 160 | tf_op jit(solution)/shard_map/ppermute | solution.py:23
  303.4 10.1 %add_bitcast_fusion = f32[2,1,256,512]{2,3,0,1:T(8,128)} fusion(s32[1,2,1,256,512]{3,4,1,2,0:T(8,128)} %copy.61, s32[1,2,1,256,512]{3,4,1,2,0:T(8,128)} %copy.60, bf16[3,304,608]{1,2,0:T(8,128)(2,1)S(1)} %get-tuple-element.339, bf16[3,256,560]{1,2,0:T(8,128)(2,1)} %get-tuple-element.343, bf16[3,256,560]{1,2,0:T(8,128)(2,1)} %get-tuple-element.342, ...), kind=kLoop, calls=%fused_computation.239 | loop fusion | flops 35913728 | bytes 16318464 | tf_op jit(solution)/shard_map/broadcast_in_dim | solution.py:241
  313.5 2.5 copy.44
  (521 shorter events, 188.2 us)
Async XLA Ops:
  1.2 233.9 %collective-permute-start.9 = (f32[2,2,1,16]{3,2,1,0:T(1,128)}, f32[2,2,1,16]{3,2,1,0:T(1,128)}, u32[]{:S(2)}, u32[]{:S(2)}) collective-permute-start(f32[2,2,1,16]{3,2,1,0:T(1,128)} %broadcast.244), channel_id=1, source_target_pairs={{0,8},{1,9},{2,10},{3,11},{4,12},{5,13},{6,14},{7,15},{8,16},{9,17... | collective-permute-start | bytes 776 | tf_op jit(solution)/shard_map/ppermute | solution.py:23
  6.2 228.9 %collective-permute-start.8 = (f32[2,2,1,16]{3,2,1,0:T(1,128)}, f32[2,2,1,16]{3,2,1,0:T(1,128)}, u32[]{:S(2)}, u32[]{:S(2)}) collective-permute-start(f32[2,2,1,16]{3,2,1,0:T(1,128)} %broadcast.244), channel_id=1, source_target_pairs={{8,0},{9,1},{10,2},{11,3},{12,4},{13,5},{14,6},{15,7},{16,8},{17,9... | collective-permute-start | bytes 776 | tf_op jit(solution)/shard_map/ppermute | solution.py:23
  8.8 22.2 %collective-permute-start.11 = (f32[2,2,8,1]{3,2,1,0:T(8,128)}, f32[2,2,8,1]{3,2,1,0:T(8,128)S(1)}, u32[]{:S(2)}, u32[]{:S(2)}) collective-permute-start(f32[2,2,8,1]{3,2,1,0:T(8,128)} %broadcast.245), channel_id=1, source_target_pairs={{0,1},{1,2},{2,3},{3,4},{4,5},{5,6},{6,7},{7,8},{8,9},{9,10},{10,1... | collective-permute-start | bytes 392 | tf_op jit(solution)/shard_map/ppermute | solution.py:23
  10.7 39.9 %collective-permute-start.10 = (f32[2,2,8,1]{3,2,1,0:T(8,128)}, f32[2,2,8,1]{3,2,1,0:T(8,128)}, u32[]{:S(2)}, u32[]{:S(2)}) collective-permute-start(f32[2,2,8,1]{3,2,1,0:T(8,128)} %broadcast.245), channel_id=1, source_target_pairs={{1,0},{2,1},{3,2},{4,3},{5,4},{6,5},{7,6},{8,7},{9,8},{10,9},{11,1... | collective-permute-start | bytes 392 | tf_op jit(solution)/shard_map/ppermute | solution.py:23
  18.3 8.7 %collective-permute-start.1 = (bf16[1,256,512]{1,2,0:T(8,128)(2,1)}, bf16[1,256,512]{1,2,0:T(8,128)(2,1)S(1)}, u32[]{:S(2)}, u32[]{:S(2)}) collective-permute-start(bf16[1,256,512]{1,2,0:T(8,128)(2,1)} %bitcast.1), channel_id=1, source_target_pairs={{64,0},{128,64},{192,128},{65,1},{129,65},{193,129},{66,2},{130,66... | collective-permute-start | bytes 786440 | tf_op jit(solution)/shard_map/ppermute | solution.py:23
  23.3 42.1 %copy-start = (bf16[2,1,256,512]{2,3,0,1:T(8,128)(2,1)}, bf16[2,1,256,512]{2,3,0,1:T(8,128)(2,1)S(1)}, u32[]{:S(2)}) copy-start(bf16[2,1,256,512]{2,3,0,1:T(8,128)(2,1)S(1)} %copy.37) | copy-start | bytes 1572868
  27.6 207.6 %collective-permute-start.6 = (f32[1,2,8,16]{3,2,1,0:T(8,128)}, f32[1,2,8,16]{3,2,1,0:T(8,128)}, u32[]{:S(2)}, u32[]{:S(2)}) collective-permute-start(f32[1,2,8,16]{3,2,1,0:T(8,128)} %broadcast.237), channel_id=1, source_target_pairs={{0,64},{64,128},{128,192},{1,65},{65,129},{129,193},{2,66},{66,130... | collective-permute-start | bytes 3080 | tf_op jit(solution)/shard_map/ppermute | solution.py:31
  31.0 7.8 %collective-permute-start.2 = (bf16[3,256,48]{1,2,0:T(8,128)(2,1)S(1)}, bf16[3,256,48]{1,2,0:T(8,128)(2,1)S(1)}, u32[]{:S(2)}, u32[]{:S(2)}) collective-permute-start(bf16[3,256,48]{1,2,0:T(8,128)(2,1)S(1)} %get-tuple-element.344), channel_id=1, source_target_pairs={{0,1},{1,2},{2,3},{3,4},{4,5},{5,6},{6,7},{7,8},{8,9},{9,10},{10,1... | collective-permute-start | bytes 221192 | tf_op jit(solution)/shard_map/ppermute | solution.py:23
  38.8 3.9 %collective-permute-start.3 = (bf16[3,256,48]{1,2,0:T(8,128)(2,1)S(1)}, bf16[3,256,48]{1,2,0:T(8,128)(2,1)S(1)}, u32[]{:S(2)}, u32[]{:S(2)}) collective-permute-start(bf16[3,256,48]{1,2,0:T(8,128)(2,1)S(1)} %get-tuple-element.345), channel_id=1, source_target_pairs={{1,0},{2,1},{3,2},{4,3},{5,4},{6,5},{7,6},{8,7},{9,8},{10,9},{11,1... | collective-permute-start | bytes 221192 | tf_op jit(solution)/shard_map/ppermute | solution.py:23
  43.0 17.1 %collective-permute-start.4 = (bf16[3,48,608]{1,2,0:T(8,128)(2,1)S(1)}, bf16[3,48,608]{1,2,0:T(8,128)(2,1)S(1)}, u32[]{:S(2)}, u32[]{:S(2)}) collective-permute-start(bf16[3,48,608]{1,2,0:T(8,128)(2,1)S(1)} %get-tuple-element.340), channel_id=1, source_target_pairs={{0,8},{1,9},{2,10},{3,11},{4,12},{5,13},{6,14},{7,15},{8,16},{9,17... | collective-permute-start | bytes 525320 | tf_op jit(solution)/shard_map/ppermute | solution.py:23
  50.6 14.9 %collective-permute-start.5 = (bf16[3,48,608]{1,2,0:T(8,128)(2,1)S(1)}, bf16[3,48,608]{1,2,0:T(8,128)(2,1)S(1)}, u32[]{:S(2)}, u32[]{:S(2)}) collective-permute-start(bf16[3,48,608]{1,2,0:T(8,128)(2,1)S(1)} %get-tuple-element.341), channel_id=1, source_target_pairs={{8,0},{9,1},{10,2},{11,3},{12,4},{13,5},{14,6},{15,7},{16,8},{17,9... | collective-permute-start | bytes 525320 | tf_op jit(solution)/shard_map/ppermute | solution.py:23
  60.1 175.1 %collective-permute-start = (f32[1,2,8,16]{3,2,1,0:T(8,128)}, f32[1,2,8,16]{3,2,1,0:T(8,128)}, u32[]{:S(2)}, u32[]{:S(2)}) collective-permute-start(f32[1,2,8,16]{3,2,1,0:T(8,128)} %broadcast.237), channel_id=1, source_target_pairs={{64,0},{128,64},{192,128},{65,1},{129,65},{193,129},{66,2},{130,66... | collective-permute-start | bytes 3080 | tf_op jit(solution)/shard_map/ppermute | solution.py:34
  228.4 6.7 %collective-permute-start.7 = (f32[1,2,8,16]{3,2,1,0:T(8,128)S(1)}, f32[1,2,8,16]{3,2,1,0:T(8,128)S(1)}, u32[]{:S(2)}, u32[]{:S(2)}) collective-permute-start(f32[1,2,8,16]{3,2,1,0:T(8,128)S(1)} %get-tuple-element.366), channel_id=1, source_target_pairs={{0,64},{64,128},{128,192},{1,65},{65,129},{129,193},{2,66},{66,130... | collective-permute-start | bytes 3080 | tf_op jit(solution)/shard_map/ppermute | solution.py:23
  235.1 68.3 %copy-start.1 = (bf16[2,1,256,512]{2,3,0,1:T(8,128)(2,1)S(1)}, bf16[2,1,256,512]{2,3,0,1:T(8,128)(2,1)}, u32[]{:S(2)}) copy-start(bf16[2,1,256,512]{2,3,0,1:T(8,128)(2,1)} %copy-done) | copy-start | bytes 1572868
  236.2 22.0 %collective-permute-start.14 = (f32[2,2,1,16]{3,2,1,0:T(1,128)S(1)}, f32[2,2,1,16]{3,2,1,0:T(1,128)S(1)}, u32[]{:S(2)}, u32[]{:S(2)}) collective-permute-start(f32[2,2,1,16]{3,2,1,0:T(1,128)S(1)} %get-tuple-element.362), channel_id=1, source_target_pairs={{8,0},{9,1},{10,2},{11,3},{12,4},{13,5},{14,6},{15,7},{16,8},{17,9... | collective-permute-start | bytes 776 | tf_op jit(solution)/shard_map/ppermute | solution.py:23
  238.1 20.1 %collective-permute-start.15 = (f32[2,2,1,16]{3,2,1,0:T(1,128)S(1)}, f32[2,2,1,16]{3,2,1,0:T(1,128)S(1)}, u32[]{:S(2)}, u32[]{:S(2)}) collective-permute-start(f32[2,2,1,16]{3,2,1,0:T(1,128)S(1)} %get-tuple-element.363), channel_id=1, source_target_pairs={{0,8},{1,9},{2,10},{3,11},{4,12},{5,13},{6,14},{7,15},{8,16},{9,17... | collective-permute-start | bytes 776 | tf_op jit(solution)/shard_map/ppermute | solution.py:23
  243.2 15.0 %collective-permute-start.12 = (f32[1,2,8,16]{3,2,1,0:T(8,128)S(1)}, f32[1,2,8,16]{3,2,1,0:T(8,128)S(1)}, u32[]{:S(2)}, u32[]{:S(2)}) collective-permute-start(f32[1,2,8,16]{3,2,1,0:T(8,128)S(1)} %get-tuple-element.360), channel_id=1, source_target_pairs={{64,0},{128,64},{192,128},{65,1},{129,65},{193,129},{66,2},{130,66... | collective-permute-start | bytes 3080 | tf_op jit(solution)/shard_map/ppermute | solution.py:34
  245.7 5.4 %collective-permute-start.16 = (f32[2,2,8,1]{3,2,1,0:T(8,128)S(1)}, f32[2,2,8,1]{3,2,1,0:T(8,128)S(1)}, u32[]{:S(2)}, u32[]{:S(2)}) collective-permute-start(f32[2,2,8,1]{3,2,1,0:T(8,128)S(1)} %get-tuple-element.364), channel_id=1, source_target_pairs={{1,0},{2,1},{3,2},{4,3},{5,4},{6,5},{7,6},{8,7},{9,8},{10,9},{11,1... | collective-permute-start | bytes 392 | tf_op jit(solution)/shard_map/ppermute | solution.py:23
  247.6 10.6 %collective-permute-start.13 = (f32[1,2,8,16]{3,2,1,0:T(8,128)S(1)}, f32[1,2,8,16]{3,2,1,0:T(8,128)S(1)}, u32[]{:S(2)}, u32[]{:S(2)}) collective-permute-start(f32[1,2,8,16]{3,2,1,0:T(8,128)S(1)} %get-tuple-element.361), channel_id=1, source_target_pairs={{0,64},{64,128},{128,192},{1,65},{65,129},{129,193},{2,66},{66,130... | collective-permute-start | bytes 3080 | tf_op jit(solution)/shard_map/ppermute | solution.py:31
  251.0 7.2 %collective-permute-start.17 = (f32[2,2,8,1]{3,2,1,0:T(8,128)S(1)}, f32[2,2,8,1]{3,2,1,0:T(8,128)S(1)}, u32[]{:S(2)}, u32[]{:S(2)}) collective-permute-start(f32[2,2,8,1]{3,2,1,0:T(8,128)S(1)} %get-tuple-element.365), channel_id=1, source_target_pairs={{0,1},{1,2},{2,3},{3,4},{4,5},{5,6},{6,7},{7,8},{8,9},{9,10},{10,1... | collective-permute-start | bytes 392 | tf_op jit(solution)/shard_map/ppermute | solution.py:23
  258.4 22.0 %collective-permute-start.20 = (f32[2,2,1,16]{3,2,1,0:T(1,128)S(1)}, f32[2,2,1,16]{3,2,1,0:T(1,128)S(1)}, u32[]{:S(2)}, u32[]{:S(2)}) collective-permute-start(f32[2,2,1,16]{3,2,1,0:T(1,128)S(1)} %get-tuple-element.356), channel_id=1, source_target_pairs={{8,0},{9,1},{10,2},{11,3},{12,4},{13,5},{14,6},{15,7},{16,8},{17,9... | collective-permute-start | bytes 776 | tf_op jit(solution)/shard_map/ppermute | solution.py:23
  260.3 20.1 %collective-permute-start.21 = (f32[2,2,1,16]{3,2,1,0:T(1,128)S(1)}, f32[2,2,1,16]{3,2,1,0:T(1,128)S(1)}, u32[]{:S(2)}, u32[]{:S(2)}) collective-permute-start(f32[2,2,1,16]{3,2,1,0:T(1,128)S(1)} %get-tuple-element.357), channel_id=1, source_target_pairs={{0,8},{1,9},{2,10},{3,11},{4,12},{5,13},{6,14},{7,15},{8,16},{9,17... | collective-permute-start | bytes 776 | tf_op jit(solution)/shard_map/ppermute | solution.py:23
  265.5 15.0 %collective-permute-start.18 = (f32[1,2,8,16]{3,2,1,0:T(8,128)S(1)}, f32[1,2,8,16]{3,2,1,0:T(8,128)S(1)}, u32[]{:S(2)}, u32[]{:S(2)}) collective-permute-start(f32[1,2,8,16]{3,2,1,0:T(8,128)S(1)} %get-tuple-element.354), channel_id=1, source_target_pairs={{64,0},{128,64},{192,128},{65,1},{129,65},{193,129},{66,2},{130,66... | collective-permute-start | bytes 3080 | tf_op jit(solution)/shard_map/ppermute | solution.py:34
  267.9 5.4 %collective-permute-start.22 = (f32[2,2,8,1]{3,2,1,0:T(8,128)S(1)}, f32[2,2,8,1]{3,2,1,0:T(8,128)S(1)}, u32[]{:S(2)}, u32[]{:S(2)}) collective-permute-start(f32[2,2,8,1]{3,2,1,0:T(8,128)S(1)} %get-tuple-element.358), channel_id=1, source_target_pairs={{1,0},{2,1},{3,2},{4,3},{5,4},{6,5},{7,6},{8,7},{9,8},{10,9},{11,1... | collective-permute-start | bytes 392 | tf_op jit(solution)/shard_map/ppermute | solution.py:23
  269.8 10.6 %collective-permute-start.19 = (f32[1,2,8,16]{3,2,1,0:T(8,128)S(1)}, f32[1,2,8,16]{3,2,1,0:T(8,128)S(1)}, u32[]{:S(2)}, u32[]{:S(2)}) collective-permute-start(f32[1,2,8,16]{3,2,1,0:T(8,128)S(1)} %get-tuple-element.355), channel_id=1, source_target_pairs={{0,64},{64,128},{128,192},{1,65},{65,129},{129,193},{2,66},{66,130... | collective-permute-start | bytes 3080 | tf_op jit(solution)/shard_map/ppermute | solution.py:31
  273.3 7.2 %collective-permute-start.23 = (f32[2,2,8,1]{3,2,1,0:T(8,128)S(1)}, f32[2,2,8,1]{3,2,1,0:T(8,128)S(1)}, u32[]{:S(2)}, u32[]{:S(2)}) collective-permute-start(f32[2,2,8,1]{3,2,1,0:T(8,128)S(1)} %get-tuple-element.359), channel_id=1, source_target_pairs={{0,1},{1,2},{2,3},{3,4},{4,5},{5,6},{6,7},{7,8},{8,9},{9,10},{10,1... | collective-permute-start | bytes 392 | tf_op jit(solution)/shard_map/ppermute | solution.py:23
  280.7 22.0 %collective-permute-start.26 = (f32[2,2,1,16]{3,2,1,0:T(1,128)S(1)}, f32[2,2,1,16]{3,2,1,0:T(1,128)S(1)}, u32[]{:S(2)}, u32[]{:S(2)}) collective-permute-start(f32[2,2,1,16]{3,2,1,0:T(1,128)S(1)} %get-tuple-element.350), channel_id=1, source_target_pairs={{8,0},{9,1},{10,2},{11,3},{12,4},{13,5},{14,6},{15,7},{16,8},{17,9... | collective-permute-start | bytes 776 | tf_op jit(solution)/shard_map/ppermute | solution.py:23
  282.6 20.1 %collective-permute-start.27 = (f32[2,2,1,16]{3,2,1,0:T(1,128)S(1)}, f32[2,2,1,16]{3,2,1,0:T(1,128)S(1)}, u32[]{:S(2)}, u32[]{:S(2)}) collective-permute-start(f32[2,2,1,16]{3,2,1,0:T(1,128)S(1)} %get-tuple-element.351), channel_id=1, source_target_pairs={{0,8},{1,9},{2,10},{3,11},{4,12},{5,13},{6,14},{7,15},{8,16},{9,17... | collective-permute-start | bytes 776 | tf_op jit(solution)/shard_map/ppermute | solution.py:23
  287.7 15.0 %collective-permute-start.24 = (f32[1,2,8,16]{3,2,1,0:T(8,128)S(1)}, f32[1,2,8,16]{3,2,1,0:T(8,128)S(1)}, u32[]{:S(2)}, u32[]{:S(2)}) collective-permute-start(f32[1,2,8,16]{3,2,1,0:T(8,128)S(1)} %get-tuple-element.348), channel_id=1, source_target_pairs={{64,0},{128,64},{192,128},{65,1},{129,65},{193,129},{66,2},{130,66... | collective-permute-start | bytes 3080 | tf_op jit(solution)/shard_map/ppermute | solution.py:34
  290.2 5.4 %collective-permute-start.28 = (f32[2,2,8,1]{3,2,1,0:T(8,128)S(1)}, f32[2,2,8,1]{3,2,1,0:T(8,128)S(1)}, u32[]{:S(2)}, u32[]{:S(2)}) collective-permute-start(f32[2,2,8,1]{3,2,1,0:T(8,128)S(1)} %get-tuple-element.352), channel_id=1, source_target_pairs={{1,0},{2,1},{3,2},{4,3},{5,4},{6,5},{7,6},{8,7},{9,8},{10,9},{11,1... | collective-permute-start | bytes 392 | tf_op jit(solution)/shard_map/ppermute | solution.py:23
  292.1 10.6 %collective-permute-start.25 = (f32[1,2,8,16]{3,2,1,0:T(8,128)S(1)}, f32[1,2,8,16]{3,2,1,0:T(8,128)S(1)}, u32[]{:S(2)}, u32[]{:S(2)}) collective-permute-start(f32[1,2,8,16]{3,2,1,0:T(8,128)S(1)} %get-tuple-element.349), channel_id=1, source_target_pairs={{0,64},{64,128},{128,192},{1,65},{65,129},{129,193},{2,66},{66,130... | collective-permute-start | bytes 3080 | tf_op jit(solution)/shard_map/ppermute | solution.py:31
  295.5 7.2 %collective-permute-start.29 = (f32[2,2,8,1]{3,2,1,0:T(8,128)S(1)}, f32[2,2,8,1]{3,2,1,0:T(8,128)S(1)}, u32[]{:S(2)}, u32[]{:S(2)}) collective-permute-start(f32[2,2,8,1]{3,2,1,0:T(8,128)S(1)} %get-tuple-element.353), channel_id=1, source_target_pairs={{0,1},{1,2},{2,3},{3,4},{4,5},{5,6},{6,7},{7,8},{8,9},{9,10},{10,1... | collective-permute-start | bytes 392 | tf_op jit(solution)/shard_map/ppermute | solution.py:23
  (57 other events, 150.0 us)
where the time goes:
time: 318 us; the launch traced here: 316 us
  matrix products  113 us (36%)
  starting transfers between devices  91.1 us (29%)
  local copies, waits for them, and re-layouts  42.7 us (13%)
  other arithmetic  30.9 us (10%)
  waiting for transfers between devices  29.6 us (9%)
  loops' own time  7.42 us (2%)
    dot_general x208, matrix products, spectral_product(): return jnp.einsum(form, left, right, preferred_element_type=jnp.float32)  113 us
    ppermute x22, starting transfers between devices, from_behind(): lax.ppermute(value, axis, [(source, source + steps) for source in range(i...  67.2 us
    ppermute x22, waiting for transfers between devices, from_behind(): lax.ppermute(value, axis, [(source, source + steps) for source in range(i...  29.6 us
    ppermute x4, starting transfers between devices, padded_2(): lax.ppermute(lax.slice_in_dim(block, block.shape[dim] - width, None, axis...  13.7 us
    dynamic_update_slice x8, local copies, waits for them, and re-layouts, section_flows(): flows = lax.map(node_row, jnp.arange(node_rows, dtype=jnp.int32))  10.7 us
    ppermute x4, starting transfers between devices, padded_2(): lax.ppermute(lax.slice_in_dim(block, 0, width, axis=dim), axis, backward)  10.2 us
    broadcast_in_dim x1, other arithmetic, shards(): return (node_mesh[:, :, None], warped[:, None])  10.1 us
    another operation x1, loops' own time, section_flows(): flows = lax.map(node_row, jnp.arange(node_rows, dtype=jnp.int32))  7.42 us
  transfers between devices with their start and end apart: 30, of which 7 were waited for; matrix products, arithmetic and copies ran while one was open for 54% of the time, Pallas kernels for 0%

commit v1 on v0

v1 whole, which is shorter than its diff:
```python
import math

import jax
import jax.numpy as jnp
import ml_dtypes
import numpy as np
from jax import lax
from jax.experimental import pallas as pl
from jax.experimental.pallas import tpu as pltpu
from jax.sharding import PartitionSpec as P

TILE_GRID = 8
PATCH = 128
STRIDE = 32
SHIFTS = 32
ITERS = 4
HALO = 48
EPS = 1e-05
STEP_RATE = 0.15
ROWS = 352
LANES = 640
OWN_LANES = 512
F32 = jnp.float32
BF16 = jnp.bfloat16


def build_tables():
    k = np.arange(PATCH)
    u = np.arange(SHIFTS) - SHIFTS // 2

    def cos_of(m):
        return np.cos(2 * np.pi * (m % PATCH) / PATCH)

    def sin_of(m):
        return np.sin(2 * np.pi * (m % PATCH) / PATCH)

    c, s = cos_of(np.outer(k, k)), sin_of(np.outer(k, k))
    gc, gs = cos_of(np.outer(u, k)), sin_of(np.outer(u, k))
    row_pass = np.zeros((2, 256, 256))
    for half in range(2):
        for w in range(2):
            start = 16 + 64 * half + 32 * w
            row_pass[half, start : start + 128, 64 * w : 64 * w + 64] = c[:, :64]
            row_pass[half, start : start + 128, 128 + 64 * w : 192 + 64 * w] = -s[:, :64]
    row_last = np.zeros((LANES, 128))
    for i in range(8):
        for j in range(16):
            lanes = (32 * j - HALO + k) % LANES
            row_last[lanes, 16 * i + j] = (-1.0) ** k
    col_pass = np.block([[c, s], [-s, c]])
    back_rows = np.block([[gc, -gs], [gs, gc]])
    factor = np.where(np.arange(64) == 0, 1.0, 2.0)[:, None]
    back_cols = np.zeros((512, 128))
    for jj in range(4):
        back_cols[64 * jj : 64 * jj + 64, 32 * jj : 32 * jj + 32] = factor * gc[:, :64].T
        back_cols[256 + 64 * jj : 320 + 64 * jj, 32 * jj : 32 * jj + 32] = -factor * gs[:, :64].T
    back_last = np.zeros((128, 512))
    for i in range(8):
        for j in range(16):
            back_last[16 * i + j, 32 * j : 32 * j + 32] = (-1.0) ** np.arange(32)
    energy_cols = np.zeros((384, 128))
    for jj in range(4):
        energy_cols[128 + 32 * jj - HALO : 256 + 32 * jj - HALO, 32 * jj : 32 * jj + 32] = 1.0
    sums = np.zeros((256, 256))
    for lane in range(128):
        jj, comp = lane % 4, (lane // 32) % 2
        sums[32 * jj : 32 * jj + 32, lane] = 1.0
        if comp == 0:
            sums[128 + 32 * jj : 160 + 32 * jj, 128 + lane] = 1.0
        else:
            sums[32 * jj : 32 * jj + 32, 128 + lane] = u
    tables = {
        "row_first": row_pass[0], "row_second": row_pass[1], "row_last": row_last, "col_pass": col_pass,
        "back_rows": back_rows, "back_cols": back_cols, "back_last": back_last, "energy_cols": energy_cols, "sums": sums,
    }
    places, pieces, base = {}, [], 0
    for name, table in tables.items():
        rows, tiles = table.shape[0], table.shape[1] // 128
        places[name] = (base, rows, tiles)
        pieces += [table[:, 128 * t : 128 * t + 128] for t in range(tiles)]
        base += rows * tiles
    packed = np.concatenate(pieces, axis=0).astype(np.float32).astype(ml_dtypes.bfloat16)
    return places, packed


PLACES, PACKED = build_tables()


class Table:
    def __init__(self, ref, name):
        self.ref = ref
        self.base, self.rows, self.tiles = PLACES[name]

    def read(self, rows=None, tiles=None):
        rows = rows or slice(0, self.rows)
        tiles = range(self.tiles) if tiles is None else tiles
        starts = [self.base + t * self.rows for t in tiles]
        parts = [self.ref[b + rows.start : b + rows.stop, :] for b in starts]
        return parts[0] if len(parts) == 1 else jnp.concatenate(parts, axis=1)


def mm(a, b):
    return jnp.dot(a, b, preferred_element_type=F32)


def split3(x):
    hi = x.astype(BF16)
    rest = x - hi.astype(F32)
    mid = rest.astype(BF16)
    low = (rest - mid.astype(F32)).astype(BF16)
    return jnp.concatenate([hi, mid, low], axis=0)


def mm_exact(x, w):
    n = x.shape[0]
    y = mm(split3(x), w)
    return y[:n] + y[n : 2 * n] + y[2 * n :]


def tile_lanes(block, t):
    if t == 0:
        return jnp.concatenate([block[:, 512:640], block[:, 0:128]], axis=1)
    return block[:, 128 * (t - 1) : 128 * (t + 1)]


def row_transform(s, pad, ri, row_pass):
    for jp in range(8):
        t, half = (jp + 1) // 2, (jp + 1) % 2
        y = mm(tile_lanes(pad[s], t), row_pass[half].read()).astype(BF16)
        ri[s, 0, :, 128 * jp : 128 * jp + 128] = y[:, :128]
        ri[s, 1, :, 128 * jp : 128 * jp + 128] = y[:, 128:]


def last_spectrum(s, pad, nq, spec_last, row_last, col_pass):
    nq[...] = mm(pad[s], row_last.read())
    lane = lax.broadcasted_iota(jnp.int32, (128, 128), 1) // 16
    picked = nq[0:128, :]
    for i in range(1, 8):
        picked = jnp.where(lane == i, nq[32 * i : 32 * i + 128, :], picked)
    spec_last[s] = mm(col_pass.read(tiles=[0]), picked.astype(BF16))


def energies(s, pad, eb, en, energy_cols):
    for b in range(11):
        x = pad[s, 32 * b : 32 * b + 32, :].astype(F32)
        eb[b : b + 1, :] = jnp.sum(x * x, axis=0, keepdims=True)
    e4 = eb[0:8, :] + eb[1:9, :] + eb[2:10, :] + eb[3:11, :]
    tiles = [e4[:, 128 * t : 128 * t + 128] for t in range(5)]
    rows = [jnp.concatenate([tiles[(q - 1) % 5], tiles[q], tiles[q + 1]], axis=1) for q in range(4)]
    y = mm_exact(jnp.concatenate(rows, axis=0), energy_cols.read())
    for q in range(4):
        en[s, q] = y[8 * q : 8 * q + 8] * (1.0 / PATCH**2) + EPS


def cross_half(x0, x1, back_rows):
    ar, ai, br, bi = x0[:128], x0[128:], x1[:128], x1[128:]
    cross = jnp.concatenate(
        [(ar * br + ai * bi).astype(BF16), (ar * bi - ai * br).astype(BF16)], axis=0
    )
    return mm(back_rows, cross)


def spectrum_of(s, i, lanes, ri, col_pass):
    rows = pl.ds(pl.multiple_of(32 * i, 32), 128)
    rhs = jnp.concatenate([ri[s, 0, rows, lanes], ri[s, 1, rows, lanes]], axis=0)
    return mm(col_pass.read(), rhs)


def store_half(half, pair, i, chunk, h):
    for t in range(2):
        half[pair, 2 * chunk + t, pl.ds(i, 64, stride=8), :] = h[:, 128 * t : 128 * t + 128]


def load_half(half, pair, rows, q):
    pieces = [half[pair, 2 * q + t, rows, :].astype(BF16) for t in range(2)]
    return jnp.concatenate(pieces, axis=1)


def first_pair(i, ri, spec, half, col_pass, back_rows):
    for chunk in range(4):
        lanes = slice(256 * chunk, 256 * chunk + 256)
        x0 = spectrum_of(0, i, lanes, ri, col_pass)
        x1 = spectrum_of(1, i, lanes, ri, col_pass)
        spec[i, :, lanes] = x1.astype(BF16)
        store_half(half, 0, i, chunk, cross_half(x0, x1, back_rows.read()))


def second_pair(i, ri, spec, half, col_pass, back_rows):
    for chunk in range(4):
        lanes = slice(256 * chunk, 256 * chunk + 256)
        x1 = spec[i, :, lanes].astype(F32)
        x2 = spectrum_of(2, i, lanes, ri, col_pass)
        store_half(half, 1, i, chunk, cross_half(x1, x2, back_rows.read()))


def pair_sums(pair, half, spec_last, en, sums_in, back_rows, back_cols, back_last):
    h_last = cross_half(spec_last[pair], spec_last[pair + 1], back_rows.read(slice(0, 32)))
    lane = lax.broadcasted_iota(jnp.int32, (8, 128), 1) // 16
    own_row = lane == lax.broadcasted_iota(jnp.int32, (8, 128), 0)
    spread = [jnp.where(own_row, h_last[u : u + 1, :], 0.0) for u in range(SHIFTS)]
    spread = jnp.concatenate(spread, axis=0).astype(BF16)
    for q in range(4):
        corr = mm(load_half(half, pair, slice(0, 256), q), back_cols.read(slice(0, 256)))
        corr += mm(load_half(half, pair, slice(256, 512), q), back_cols.read(slice(256, 512)))
        corr += mm(spread, back_last.read(tiles=[q]))
        scale = (PATCH / 2.0 / PATCH**4) * lax.rsqrt(en[pair, q] * en[pair + 1, q])
        total = jnp.zeros((8, 128), F32)
        along = jnp.zeros((8, 128), F32)
        for u in range(SHIFTS):
            w = jnp.exp(corr[8 * u : 8 * u + 8] * scale)
            total += w
            along += w * float(u - SHIFTS // 2)
        sums_in[32 * pair + 8 * q : 32 * pair + 8 * q + 8, 0:128] = total
        sums_in[32 * pair + 8 * q : 32 * pair + 8 * q + 8, 128:256] = along


def flow_block(sums_in, sums, last_sec):
    y = mm_exact(sums_in[...], sums.read())
    flow = y[:, 128:] / y[:, :128]
    lane = lax.broadcasted_iota(jnp.int32, (8, 128), 1)
    block = jnp.zeros((8, 128), F32)
    for pair in range(2):
        for q in range(4):
            first = 8 + 4 * q
            mine = (lane // 64 == pair) & (lane % 32 >= first) & (lane % 32 < first + 4)
            r = 32 * pair + 8 * q
            block = jnp.where(mine, flow[r : r + 8], block)
    return jnp.where((lane >= 64) & last_sec, 0.0, block)


def extend(own, left, right):
    lane = lax.broadcasted_iota(jnp.int32, own.shape, own.ndim - 1) % 32
    from_left = pltpu.roll(left, 112, own.ndim - 1)
    from_right = pltpu.roll(right, 16, own.ndim - 1)
    return jnp.where(lane < 8, from_left, jnp.where(lane >= 24, from_right, own))


def relax(flow, row_pos, col_pos):
    shape = flow[0].shape
    row = lax.broadcasted_iota(jnp.int32, shape, 0)
    lane = lax.broadcasted_iota(jnp.int32, shape, 1)
    node = lane % 32
    inside = ((row >= 8) | (row_pos > 0)) & ((row < 16) | (row_pos < TILE_GRID - 1))
    inside &= ((node >= 8) | (col_pos > 0)) & ((node < 24) | (col_pos < TILE_GRID - 1))
    mask = jnp.where(inside, 1.0, 0.0)
    low = lane < 64
    count = len(flow)
    zero = jnp.zeros(shape, F32)

    def following(f):
        turned = [pltpu.roll(x, 64, 1) for x in f] + [zero]
        return [jnp.where(low, turned[d], turned[d + 1]) for d in range(count)]

    def preceding(f):
        turned = [zero] + [pltpu.roll(x, 64, 1) for x in f]
        return [jnp.where(low, turned[d], turned[d + 1]) for d in range(count)]

    flow = [f * mask for f in flow]
    mesh = [zero] * count
    for step in range(ITERS):
        if step == 0:
            spring = [-f for f in flow]
        else:
            spring = [m - n - f for m, n, f in zip(mesh, following(mesh), flow)]
        earlier = preceding(spring)
        updated = []
        for m, sp, ea in zip(mesh, spring, earlier):
            change = sp - ea
            if step > 0:
                around = pltpu.roll(m, 1, 0) + pltpu.roll(m, 23, 0) + pltpu.roll(m, 1, 1) + pltpu.roll(m, 127, 1)
                change = change + 4.0 * m - around
            updated.append((m - STEP_RATE * change) * mask)
        mesh = updated
    return mesh


def pick_four(code, values):
    low = jnp.where(code == -2, values[0], values[1])
    high = jnp.where(code == 0, values[2], values[3])
    return jnp.where(code < 0, low, high)


def shifted_columns(s, r, pad, cols):
    x = pad[s, pl.ds(pl.multiple_of(32 * r + 32, 32), 64), :].astype(F32)[8:56]
    for d in range(5):
        y = x if d == 2 else pltpu.roll(x, (2 - d) % LANES, 1)
        cols[d] = y[:, :OWN_LANES]


def corners(s, r, offsets, cols, coef):
    band = pl.ds(pl.multiple_of(32 * r, 32), 32)
    for q in range(4):
        lanes = slice(128 * q, 128 * q + 128)
        ro = offsets[0, s, 0, band, lanes]
        co = offsets[1, s, 0, band, lanes]
        left, right = [], []
        for dr in range(-2, 3):
            v = [cols[d, 8 + dr : 40 + dr, lanes] for d in range(5)]
            left.append(pick_four(co, v[0:4]))
            right.append(pick_four(co, v[1:5]))
        i00, i10 = pick_four(ro, left[0:4]), pick_four(ro, left[1:5])
        i01, i11 = pick_four(ro, right[0:4]), pick_four(ro, right[1:5])
        rf, cf = ro.astype(F32), co.astype(F32)
        top, low = i01 - i00, i11 - i10
        top0, low0 = i00 - cf * top, i10 - cf * low
        twist, lean = low - top, low0 - top0
        coef[0, s, band, lanes] = top0 - rf * lean
        coef[1, s, band, lanes] = lean
        coef[2, s, band, lanes] = top - rf * twist
        coef[3, s, band, lanes] = twist


def write_mesh(mesh, out):
    for s in range(2):
        for c in range(2):
            lane = 64 * s + 32 * c + 8
            out[s, c, 0] = mesh[:, lane : lane + 16]


def spread_lanes(mesh, s, c, q):
    lane = lax.broadcasted_iota(jnp.int32, (8, 128), 1)
    return jnp.take_along_axis(mesh, 64 * s + 32 * c + 8 + 4 * q + lane // 32, axis=1)


def blend(s, mesh, coef, out):
    for q in range(4):
        lanes = slice(128 * q, 128 * q + 128)
        mr, mc = spread_lanes(mesh, s, 0, q), spread_lanes(mesh, s, 1, q)
        for r in range(8):
            band = slice(32 * r, 32 * r + 32)
            a, b = mr[r : r + 1], mc[r : r + 1]
            first = coef[0, s, band, lanes] + a * coef[1, s, band, lanes]
            second = coef[2, s, band, lanes] + a * coef[3, s, band, lanes]
            out[s, 0, band, lanes] = first + b * second


MESH = pl.DeviceIdType.MESH
AROUND = [(0, -1), (0, 1), (-1, 0), (1, 0), (-1, -1), (-1, 1), (1, -1), (1, 1)]


def pixel_part(dr, dc, sections, pad, from_left, from_right, src, dst):
    src_rows = {-1: pl.ds(0, HALO), 0: pl.ds(0, 256), 1: pl.ds(256 - HALO, HALO)}[dr]
    dst_rows = {-1: pl.ds(HALO + 256, HALO), 0: pl.ds(HALO, 256), 1: pl.ds(0, HALO)}[dr]
    if dc == 0:
        return sections.at[src, 0, src_rows, :], pad.at[dst, dst_rows, pl.ds(0, OWN_LANES)]
    if dc < 0:
        return sections.at[src, 0, src_rows, pl.ds(0, 128)], from_right.at[dst, dst_rows, :]
    return sections.at[src, 0, src_rows, pl.ds(OWN_LANES - 128, 128)], from_left.at[dst, dst_rows, :]


def merge_sides(s, rows, pad, from_left, from_right, col_pos):
    lane = lax.broadcasted_iota(jnp.int32, (rows.stop - rows.start, 128), 1)
    side = jnp.where(lane < 64, from_right[s, rows, :].astype(F32), from_left[s, rows, :].astype(F32))
    keep = ((lane < 64) & (col_pos < TILE_GRID - 1)) | ((lane >= 64) & (col_pos > 0))
    pad[s, rows, OWN_LANES:LANES] = jnp.where(keep, side, 0.0).astype(BF16)


def clear_edges(first, count, pad, row_pos):
    @pl.when(row_pos == 0)
    def _():
        pad[first : first + count, 0:HALO, :] = jnp.zeros((count, HALO, LANES), BF16)

    @pl.when(row_pos == TILE_GRID - 1)
    def _():
        pad[first : first + count, ROWS - HALO : ROWS, :] = jnp.zeros((count, HALO, LANES), BF16)


def whole_kernel(sections, offsets_in, packed, mesh_out, warped,
                 pad, from_left, from_right, offsets, ri, spec, half, nq, spec_last, eb, en, sums_in, flows, cols, coef,
                 local_sem, pixel_send, pixel_recv, sec_send, sec_recv, near_send, near_recv):
    row_pass = [Table(packed, "row_first"), Table(packed, "row_second")]
    row_last, col_pass, back_rows, back_cols, back_last, energy_cols, sums = (
        Table(packed, name)
        for name in ("row_last", "col_pass", "back_rows", "back_cols", "back_last", "energy_cols", "sums")
    )
    sec, tile = lax.axis_index("sec"), lax.axis_index("tile")
    sec_count = lax.axis_size("sec")
    row_pos, col_pos = tile // TILE_GRID, tile % TILE_GRID

    def device(ds, dr, dc):
        row = lax.rem(row_pos + (dr + TILE_GRID), TILE_GRID)
        col = lax.rem(col_pos + (dc + TILE_GRID), TILE_GRID)
        return (lax.rem(sec + ds, sec_count), row * TILE_GRID + col)

    own_copy = pltpu.make_async_copy(
        sections.at[:, 0], pad.at[pl.ds(0, 2), pl.ds(HALO, 256), pl.ds(0, OWN_LANES)], local_sem.at[0]
    )
    offset_copy = pltpu.make_async_copy(offsets_in, offsets, local_sem.at[1])
    own_copy.start()
    offset_copy.start()

    barrier = pltpu.get_barrier_semaphore()
    partners = [(0, dr, dc) for dr, dc in AROUND] + [(2, 0, 0)]
    partners += [(ds, dr, dc) for ds in (1, 3) for dr, dc in AROUND + [(0, 0)]]
    for p in partners:
        pl.semaphore_signal(barrier, inc=1, device_id=device(*p), device_id_type=MESH)
    pl.semaphore_wait(barrier, len(partners))

    def pixel_copy(k, ds, dr, dc, src, dst):
        src_ref, dst_ref = pixel_part(dr, dc, sections, pad, from_left, from_right, src, dst)
        return pltpu.make_async_remote_copy(
            src_ref=src_ref, dst_ref=dst_ref, send_sem=pixel_send.at[k], recv_sem=pixel_recv.at[k],
            device_id=device(ds, dr, dc), device_id_type=MESH,
        )

    both, first, third = pl.ds(0, 2), pl.ds(0, 1), pl.ds(2, 1)
    own = [pixel_copy(k, 0, dr, dc, both, both) for k, (dr, dc) in enumerate(AROUND)]
    after = [pixel_copy(8 + k, 3, dr, dc, first, third) for k, (dr, dc) in enumerate([(0, 0)] + AROUND)]
    for copy in own + after:
        copy.start()

    def bands(s, start, step, count):
        @pl.loop(0, count)
        def _(k):
            r = start + step * k
            shifted_columns(s, r, pad, cols)
            corners(s, r, offsets, cols, coef)

    own_copy.wait()
    own[0].wait_recv()
    own[1].wait_recv()
    offset_copy.wait()
    for s in range(2):
        merge_sides(s, slice(HALO, HALO + 256), pad, from_left, from_right, col_pos)
        bands(s, 1, 1, 6)
    for copy in own[2:]:
        copy.wait_recv()
    for s in range(2):
        merge_sides(s, slice(0, HALO), pad, from_left, from_right, col_pos)
        merge_sides(s, slice(HALO + 256, ROWS), pad, from_left, from_right, col_pos)
    clear_edges(0, 2, pad, row_pos)

    def transform(s):
        row_transform(s, pad, ri, row_pass)
        last_spectrum(s, pad, nq, spec_last, row_last, col_pass)
        energies(s, pad, eb, en, energy_cols)

    transform(0)
    transform(1)

    @pl.loop(0, 8)
    def _(i):
        first_pair(i, ri, spec, half, col_pass, back_rows)

    for copy in after:
        copy.wait_recv()
    merge_sides(2, slice(0, ROWS), pad, from_left, from_right, col_pos)
    clear_edges(2, 1, pad, row_pos)
    transform(2)

    @pl.loop(0, 8)
    def _(i):
        second_pair(i, ri, spec, half, col_pass, back_rows)

    for pair in range(2):
        pair_sums(pair, half, spec_last, en, sums_in, back_rows, back_cols, back_last)
    flows[4, sec] = flow_block(sums_in, sums, sec == sec_count - 1)

    along = [
        pltpu.make_async_remote_copy(
            src_ref=flows.at[4, sec], dst_ref=flows.at[4, sec], send_sem=sec_send.at[ds - 1],
            recv_sem=sec_recv.at[ds - 1], device_id=device(ds, 0, 0), device_id_type=MESH,
        )
        for ds in (1, 2, 3)
    ]
    for copy in along:
        copy.start()
    bands(0, 0, 7, 2)
    for copy in along:
        copy.wait_recv()
    beside = [
        pltpu.make_async_remote_copy(
            src_ref=flows.at[4], dst_ref=flows.at[3 * (1 - dr) + 1 - dc], send_sem=near_send.at[k],
            recv_sem=near_recv.at[k], device_id=device(0, dr, dc), device_id_type=MESH,
        )
        for k, (dr, dc) in enumerate(AROUND)
    ]
    for copy in beside:
        copy.start()
    bands(1, 0, 7, 2)
    for copy in beside:
        copy.wait_recv()

    def column(d, c):
        return jnp.concatenate([flows[c, d], flows[3 + c, d], flows[6 + c, d]], axis=0)

    mesh = relax([extend(column(d, 1), column(d, 0), column(d, 2)) for d in range(4)], row_pos, col_pos)
    mine = mesh[0][8:16]
    for d in range(1, 4):
        mine = jnp.where(sec == d, mesh[d][8:16], mine)
    write_mesh(mine, mesh_out)
    for s in range(2):
        blend(s, mine, coef, warped)
    for copy in own + after + along + beside:
        copy.wait_send()


def vmem():
    return pl.BlockSpec(memory_space=pltpu.VMEM)


def shards(sections, corner_offsets):
    anywhere = pl.BlockSpec(memory_space=pl.ANY)
    dma = pltpu.SemaphoreType.DMA
    return pl.pallas_call(
        whole_kernel,
        out_shape=(
            jax.ShapeDtypeStruct((2, 2, 1, 8, 16), F32),
            jax.ShapeDtypeStruct((2, 1, 256, 512), F32),
        ),
        in_specs=[anywhere, anywhere, vmem()],
        out_specs=(vmem(), vmem()),
        scratch_shapes=[
            pltpu.VMEM((3, ROWS, LANES), BF16),
            pltpu.VMEM((3, ROWS, 128), BF16),
            pltpu.VMEM((3, ROWS, 128), BF16),
            pltpu.VMEM((2, 2, 1, 256, OWN_LANES), jnp.int32),
            pltpu.VMEM((3, 2, ROWS, 1024), BF16),
            pltpu.VMEM((8, 256, 1024), BF16),
            pltpu.VMEM((2, 8, 512, 128), F32),
            pltpu.VMEM((ROWS, 128), F32),
            pltpu.VMEM((3, 256, 128), F32),
            pltpu.VMEM((16, LANES), F32),
            pltpu.VMEM((3, 4, 8, 128), F32),
            pltpu.VMEM((64, 256), F32),
            pltpu.VMEM((9, 4, 8, 128), F32),
            pltpu.VMEM((5, 48, OWN_LANES), F32),
            pltpu.VMEM((4, 2, 256, OWN_LANES), F32),
            dma((2,)),
            dma((17,)),
            dma((17,)),
            dma((3,)),
            dma((3,)),
            dma((8,)),
            dma((8,)),
        ],
        compiler_params=pltpu.CompilerParams(
            vmem_limit_bytes=60 * 2**20, collective_id=0, has_side_effects=True
        ),
    )(sections, corner_offsets, jnp.asarray(PACKED))


def solution(mesh):
    in_specs = (P("sec", "tile", None, None), P(None, "sec", "tile", None, None))
    out_specs = (P("sec", None, "tile", None, None), P("sec", "tile", None, None))
    return jax.shard_map(shards, mesh=mesh, in_specs=in_specs, out_specs=out_specs, check_vma=False)
```

time: 318 us -> 56.7 us (0.18)
  the two profiles are of different devices: /device:TPU:98 before, /device:TPU:1 now
where the time goes in v1:
time: 56.7 us; the launch traced here: 56.5 us
  Pallas kernels  52.3 us (92%)
  local copies, waits for them, and re-layouts  3.59 us (6%)
  between operations  0.64 us (1%)
    pallas_call x1, Pallas kernels, shards(): pl.pallas_call(whole_kernel, out_shape=(jax.ShapeDtypeStruct((2, 2, 1, 8,...  52.3 us
    unnamed x2, local copies, waits for them, and re-layouts  3.59 us

profile of v1, /device:TPU:1, one launch (start us, length us, event | category | flops | bytes accessed | tf_op | source)
XLA Modules:
  0.0 56.5 jit_solution(6603856792150549976)
XLA Ops:
  0.6 52.3 %shard_map.50 = (f32[2,2,1,8,16]{4,3,2,1,0:T(8,128)}, f32[2,1,256,512]{3,2,1,0:T(8,128)}) custom-call(bf16[2,1,256,512]{3,2,1,0:T(8,128)(2,1)} %sections.1, s32[2,2,1,256,512]{4,3,2,1,0:T(8,128)} %offsets_in.1, bf16[4224,128]{1,0:T(8,128)(2,1)} %constant.2.clone.packed), custom_call_target="tpu_custom_call" | custom-call | tf_op jit(solution)/shard_map/pallas_call | solution.py:505
  52.9 1.3 %copy.7 = f32[2,2,1,8,16]{4,3,2,1,0:T(8,128)} copy(f32[2,2,1,8,16]{4,3,2,1,0:T(8,128)} %get-tuple-element.4) | data formatting | bytes 4096
  54.3 2.3 %copy.8 = f32[2,1,256,512]{3,2,1,0:T(8,128)} copy(f32[2,1,256,512]{3,2,1,0:T(8,128)} %get-tuple-element.5) | data formatting | bytes 2097152

commit v2 on v1

v2 whole, which is shorter than its diff:
```python
import math

import jax
import jax.numpy as jnp
import ml_dtypes
import numpy as np
from jax import lax
from jax.experimental import pallas as pl
from jax.experimental.pallas import tpu as pltpu
from jax.sharding import PartitionSpec as P

TILE_GRID = 8
PATCH = 128
STRIDE = 32
SHIFTS = 32
ITERS = 4
HALO = 48
EPS = 1e-05
STEP_RATE = 0.15
ROWS = 352
LANES = 640
OWN_LANES = 512
F32 = jnp.float32
BF16 = jnp.bfloat16


def build_tables():
    k = np.arange(PATCH)
    u = np.arange(SHIFTS) - SHIFTS // 2

    def cos_of(m):
        return np.cos(2 * np.pi * (m % PATCH) / PATCH)

    def sin_of(m):
        return np.sin(2 * np.pi * (m % PATCH) / PATCH)

    c, s = cos_of(np.outer(k, k)), sin_of(np.outer(k, k))
    gc, gs = cos_of(np.outer(u, k)), sin_of(np.outer(u, k))
    factor = np.where(k[:64] == 0, 1.0, 2.0)
    first = []
    for count, shift, slot in ((4, 16, 0), (2, 0, 0), (2, 96, 2)):
        table = np.zeros((128 * count + 16, 256))
        for i in range(count):
            rows = slice(32 * i + shift, 32 * i + shift + 128)
            table[i : 64 * count : count, rows] = c[:64]
            table[64 * count + i : 128 * count : count, rows] = -s[:64]
            table[128 * count + slot + i, rows] = (-1.0) ** k
        first.append(table)
    second = np.block([[c, -s], [s, c]])
    back_second = np.zeros((1024, 256))
    for w in range(4):
        rows, lanes = 256 * w, 32 * w
        back_second[rows : rows + 128, lanes : lanes + 32] = gc.T
        back_second[rows + 128 : rows + 256, lanes : lanes + 32] = -gs.T
        back_second[rows : rows + 128, 128 + lanes : 160 + lanes] = gs.T
        back_second[rows + 128 : rows + 256, 128 + lanes : 160 + lanes] = gc.T
    inner, outer = np.zeros((128, 512)), np.zeros((128, 512))
    for i in range(4):
        inner[i::4, i:256:4] = factor * gc[:, :64]
        inner[i::4, 256 + i : 512 : 4] = -factor * gs[:, :64]
        start = 128 * (i // 2) + i % 2
        outer[i::4, start : 128 * (i // 2) + 128 : 2] = factor * gc[:, :64]
        outer[i::4, 256 + start : 384 + 128 * (i // 2) : 2] = -factor * gs[:, :64]
    energy_cols = np.zeros((384, 128))
    for jj in range(4):
        energy_cols[128 + 32 * jj - HALO : 256 + 32 * jj - HALO, 32 * jj : 32 * jj + 32] = 1.0
    sums = np.zeros((256, 256))
    for lane in range(128):
        jj, comp = lane % 4, (lane // 32) % 2
        sums[32 * jj : 32 * jj + 32, lane] = 1.0
        if comp == 0:
            sums[128 + 32 * jj : 160 + 32 * jj, 128 + lane] = 1.0
        else:
            sums[32 * jj : 32 * jj + 32, 128 + lane] = u
    tables = {
        "inner": first[0], "upper": first[1], "lower": first[2], "second": second, "back_second": back_second,
        "back_first": np.concatenate([inner, outer], axis=0), "energy_cols": energy_cols, "sums": sums,
    }
    places, pieces, base = {}, [], 0
    for name, table in tables.items():
        rows, tiles = table.shape[0], table.shape[1] // 128
        places[name] = (base, rows, tiles)
        pieces += [table[:, 128 * t : 128 * t + 128] for t in range(tiles)]
        base += rows * tiles
    packed = np.concatenate(pieces, axis=0).astype(np.float32).astype(ml_dtypes.bfloat16)
    return places, packed


PLACES, PACKED = build_tables()


class Table:
    def __init__(self, ref, name):
        self.ref = ref
        self.base, self.rows, self.tiles = PLACES[name]

    def read(self, rows=None, tiles=None):
        rows = rows or slice(0, self.rows)
        tiles = range(self.tiles) if tiles is None else tiles
        starts = [self.base + t * self.rows for t in tiles]
        parts = [self.ref[b + rows.start : b + rows.stop, :] for b in starts]
        return parts[0] if len(parts) == 1 else jnp.concatenate(parts, axis=1)

    def read_part(self, part, rows):
        starts = [self.base + t * self.rows for t in range(self.tiles)]
        parts = [self.ref[pl.ds(pl.multiple_of(b + part * rows, 16), rows), :] for b in starts]
        return jnp.concatenate(parts, axis=1)


def mm(a, b):
    return jnp.dot(a, b, preferred_element_type=F32)


def split3(x):
    hi = x.astype(BF16)
    rest = x - hi.astype(F32)
    mid = rest.astype(BF16)
    low = (rest - mid.astype(F32)).astype(BF16)
    return jnp.concatenate([hi, mid, low], axis=0)


def mm_exact(x, w):
    n = x.shape[0]
    y = mm(split3(x), w)
    return y[:n] + y[n : 2 * n] + y[2 * n :]


def block_energies(s, blocks, lanes, pad, eb):
    for b in blocks:
        x = pad[s, 32 * b : 32 * b + 32, lanes].astype(F32)
        eb[s, b : b + 1, lanes] = jnp.sum(x * x, axis=0, keepdims=True)


def node_energies(s, columns, eb, en, energy_cols):
    e4 = eb[s, 0:8, :] + eb[s, 1:9, :] + eb[s, 2:10, :] + eb[s, 3:11, :]
    tiles = [e4[:, 128 * t : 128 * t + 128] for t in range(5)]
    rows = [jnp.concatenate([tiles[(q - 1) % 5], tiles[q], tiles[q + 1]], axis=1) for q in columns]
    y = mm_exact(jnp.concatenate(rows, axis=0), energy_cols.read())
    row = lax.broadcasted_iota(jnp.int32, (8, 128), 0)
    for n, q in enumerate(columns):
        e = y[8 * n : 8 * n + 8] * (1.0 / PATCH**2) + EPS
        en[s, INNER, q] = jnp.where(row < 4, pltpu.roll(e, 6, 0), pltpu.roll(e, 2, 0))
        en[s, OUTER, q] = jnp.where((row < 2) | (row >= 6), e, pltpu.roll(e, 4, 0))


INNER, OUTER = 0, 1
OWN_COLS, SIDE_COLS = (slice(0, 256), slice(256, 512)), (slice(512, 640),)


def first_transform(s, group, columns, pad, spec, tables):
    for lanes in columns:
        if group == INNER:
            parts = [(0, 256, mm(tables["inner"].read(), pad[s, HALO : HALO + 256, lanes]))]
        else:
            parts = [
                (0, 128, mm(tables["upper"].read(), pad[s, 0:256, lanes])),
                (128, 128, mm(tables["lower"].read(), pad[s, 96:352, lanes])),
            ]
        for n in range((lanes.stop - lanes.start) // 128):
            t = (lanes.start // 128 + n + 1) % 5
            cols = slice(128 * n, 128 * n + 128)
            last = None
            for row, count, y in parts:
                spec[s, group, t, 0, row : row + count, :] = y[0:count, cols].astype(BF16)
                spec[s, group, t, 1, row : row + count, :] = y[count : 2 * count, cols].astype(BF16)
                end = y[2 * count : 2 * count + 16, cols]
                last = end if last is None else last + end
            spec[s, group, t, 0, 256:272, :] = last.astype(BF16)
            spec[s, group, t, 1, 256:272, :] = jnp.zeros((16, 128), BF16)


def window(s, group, q, w, spec):
    start = 32 * w - HALO
    before = lax.rem(q + (1 if start >= 0 else 0), 5)
    after = lax.rem(before + 1, 5)
    lane = lax.broadcasted_iota(jnp.int32, (272, 128), 1)
    parts = []
    for part in range(2):
        parts.append(jnp.where(lane < start % 128, spec[s, group, after, part], spec[s, group, before, part]))
    return jnp.concatenate(parts, axis=1)


def cross(x0, x1):
    ar, ai, br, bi = x0[:, :128], x0[:, 128:], x1[:, :128], x1[:, 128:]
    return jnp.concatenate([(ar * br + ai * bi).astype(BF16), (ar * bi - ai * br).astype(BF16)], axis=1)


def unit_of(n):
    m = lax.rem(n, 4)
    return n // 8, lax.rem(n // 4, 2), lax.rem(m + 1, 3) + 2 * (m // 3)


def cross_unit(pair, n, spec, kept, crossed, tables):
    _, group, q = unit_of(n)
    for w in range(4):
        x1 = mm(window(pair + 1, group, q, w, spec), tables["second"].read())
        if pair == 0:
            x0 = mm(window(0, group, q, w, spec), tables["second"].read())
            kept[group, q, w] = x1.astype(BF16)
        else:
            x0 = kept[group, q, w].astype(F32)
        crossed[:, 256 * w : 256 * w + 256] = cross(x0, x1)


def columns_back(crossed, turned, last_row, tables):
    back = mm(crossed[...], tables["back_second"].read())
    turned[0:256, :] = back[0:256, :128].astype(BF16)
    turned[256:512, :] = back[0:256, 128:].astype(BF16)
    last = back[256:264, 0:128]
    low = lax.broadcasted_iota(jnp.int32, (8, 128), 0) < 4
    last_row[...] = jnp.where(low, last, -pltpu.roll(last, 4, 0))


def rows_back(n, turned, last_row, en, unit_sums, tables):
    pair, group, q = unit_of(n)
    corr = mm(tables["back_first"].read_part(group, 128), turned[...])
    low = lax.broadcasted_iota(jnp.int32, (8, 128), 0) < 4
    scale = (PATCH / 2.0 / PATCH**4) * lax.rsqrt(en[pair, group, q] * en[pair + 1, group, q])
    last = last_row[...]
    total = jnp.zeros((8, 128), F32)
    along = jnp.zeros((8, 128), F32)
    for u in range(0, SHIFTS, 2):
        weight = jnp.exp((corr[4 * u : 4 * u + 8] + last) * scale)
        total += weight
        along += weight * jnp.where(low, float(u - SHIFTS // 2), float(u + 1 - SHIFTS // 2))
    unit_sums[n, :, 0:128] = total + pltpu.roll(total, 4, 0)
    unit_sums[n, :, 128:256] = along + pltpu.roll(along, 4, 0)


def flow_block(unit_sums, sums, last_sec):
    row = lax.broadcasted_iota(jnp.int32, (8, 256), 0)
    pieces = []
    for pair in range(2):
        for q in range(4):
            m = (2, 0, 1, 3)[q]
            inner, outer = unit_sums[8 * pair + m], unit_sums[8 * pair + 4 + m]
            pieces.append(jnp.where((row >= 2) & (row < 6), pltpu.roll(inner, 2, 0), outer))
    y = mm_exact(jnp.concatenate(pieces, axis=0), sums.read())
    flow = y[:, 128:] / y[:, :128]
    lane = lax.broadcasted_iota(jnp.int32, (8, 128), 1)
    block = jnp.zeros((8, 128), F32)
    for pair in range(2):
        for q in range(4):
            first = 8 + 4 * q
            mine = (lane // 64 == pair) & (lane % 32 >= first) & (lane % 32 < first + 4)
            r = 32 * pair + 8 * q
            block = jnp.where(mine, flow[r : r + 8], block)
    return jnp.where((lane >= 64) & last_sec, 0.0, block)


def extend(own, left, right):
    lane = lax.broadcasted_iota(jnp.int32, own.shape, own.ndim - 1) % 32
    from_left = pltpu.roll(left, 112, own.ndim - 1)
    from_right = pltpu.roll(right, 16, own.ndim - 1)
    return jnp.where(lane < 8, from_left, jnp.where(lane >= 24, from_right, own))


def relax(flow, row_pos, col_pos):
    shape = flow[0].shape
    row = lax.broadcasted_iota(jnp.int32, shape, 0)
    lane = lax.broadcasted_iota(jnp.int32, shape, 1)
    node = lane % 32
    inside = ((row >= 8) | (row_pos > 0)) & ((row < 16) | (row_pos < TILE_GRID - 1))
    inside &= ((node >= 8) | (col_pos > 0)) & ((node < 24) | (col_pos < TILE_GRID - 1))
    mask = jnp.where(inside, 1.0, 0.0)
    low = lane < 64
    count = len(flow)
    zero = jnp.zeros(shape, F32)

    def following(f):
        turned = [pltpu.roll(x, 64, 1) for x in f] + [zero]
        return [jnp.where(low, turned[d], turned[d + 1]) for d in range(count)]

    def preceding(f):
        turned = [zero] + [pltpu.roll(x, 64, 1) for x in f]
        return [jnp.where(low, turned[d], turned[d + 1]) for d in range(count)]

    flow = [f * mask for f in flow]
    mesh = [zero] * count
    for step in range(ITERS):
        if step == 0:
            spring = [-f for f in flow]
        else:
            spring = [m - n - f for m, n, f in zip(mesh, following(mesh), flow)]
        earlier = preceding(spring)
        updated = []
        for m, sp, ea in zip(mesh, spring, earlier):
            change = sp - ea
            if step > 0:
                around = pltpu.roll(m, 1, 0) + pltpu.roll(m, 23, 0) + pltpu.roll(m, 1, 1) + pltpu.roll(m, 127, 1)
                change = change + 4.0 * m - around
            updated.append((m - STEP_RATE * change) * mask)
        mesh = updated
    return mesh


SHIFT_ROWS = 288


def shifted_columns(pad, cols):
    @pl.loop(0, SHIFT_ROWS // 16)
    def _(k):
        for s in range(2):
            x = pad[s, pl.ds(pl.multiple_of(32 + 16 * k, 16), 16), :].astype(F32)
            for d in range(5):
                y = x if d == 2 else pltpu.roll(x, (2 - d) % LANES, 1)
                for t in range(4):
                    cols[d, pl.ds(128 * k + (4 * s + t), 16, stride=8), :] = y[:, 128 * t : 128 * t + 128]


def pick_pair(high, odd, values):
    near = [jnp.where(high, values[k + 2], values[k]) for k in range(3)]
    return jnp.where(odd, near[1], near[0]), jnp.where(odd, near[2], near[1])


def corners(r, offsets, by_row, cols, coef):
    base = pl.multiple_of(8 * r, 8)
    for c in range(2):
        for st in range(8):
            by_row[c, pl.ds(st, 8, stride=8), :] = offsets[c, pl.ds(pl.multiple_of(256 * st + base, 8), 8), :]
    view = [
        [cols[d, pl.ds(pl.multiple_of(8 * base + 8 * (14 + k), 8), 8), :] for d in range(5)] for k in range(12)
    ]
    for k in range(8):
        ro = by_row[0, 8 * k : 8 * k + 8, :]
        co = by_row[1, 8 * k : 8 * k + 8, :]
        row_high, row_odd = ro >= 0, (ro & 1) == 1
        col_high, col_odd = co >= 0, (co & 1) == 1
        pairs = [pick_pair(col_high, col_odd, view[k + dr]) for dr in range(5)]
        i00, i10 = pick_pair(row_high, row_odd, [p[0] for p in pairs])
        i01, i11 = pick_pair(row_high, row_odd, [p[1] for p in pairs])
        rf, cf = ro.astype(F32), co.astype(F32)
        top, low = i01 - i00, i11 - i10
        top0, low0 = i00 - cf * top, i10 - cf * low
        twist, lean = low - top, low0 - top0
        coef[0, base + k] = top0 - rf * lean
        coef[1, base + k] = lean
        coef[2, base + k] = top - rf * twist
        coef[3, base + k] = twist


def write_mesh(mesh, out):
    for s in range(2):
        for c in range(2):
            lane = 64 * s + 32 * c + 8
            out[s, c, 0] = mesh[:, lane : lane + 16]


def spread_lanes(mesh, i, c):
    tile = lax.broadcasted_iota(jnp.int32, (8, 128), 0)
    lane = lax.broadcasted_iota(jnp.int32, (8, 128), 1)
    place = 64 * (tile // 4) + 4 * (tile % 4) + lane // 32 + (32 * c + 8)
    return jnp.take_along_axis(jnp.broadcast_to(mesh[i : i + 1], (8, 128)), place, axis=1)


MESH = pl.DeviceIdType.MESH
AROUND = [(0, -1), (0, 1), (-1, 0), (1, 0), (-1, -1), (-1, 1), (1, -1), (1, 1)]


def pixel_part(dr, dc, sections, pad, from_left, from_right, src, dst):
    src_rows = {-1: pl.ds(0, HALO), 0: pl.ds(0, 256), 1: pl.ds(256 - HALO, HALO)}[dr]
    dst_rows = {-1: pl.ds(HALO + 256, HALO), 0: pl.ds(HALO, 256), 1: pl.ds(0, HALO)}[dr]
    if dc == 0:
        return sections.at[src, 0, src_rows, :], pad.at[dst, dst_rows, pl.ds(0, OWN_LANES)]
    if dc < 0:
        return sections.at[src, 0, src_rows, pl.ds(0, 128)], from_right.at[dst, dst_rows, :]
    return sections.at[src, 0, src_rows, pl.ds(OWN_LANES - 128, 128)], from_left.at[dst, dst_rows, :]


def merge_sides(s, rows, pad, from_left, from_right, col_pos):
    lane = lax.broadcasted_iota(jnp.int32, (rows.stop - rows.start, 128), 1)
    side = jnp.where(lane < 64, from_right[s, rows, :].astype(F32), from_left[s, rows, :].astype(F32))
    keep = ((lane < 64) & (col_pos < TILE_GRID - 1)) | ((lane >= 64) & (col_pos > 0))
    pad[s, rows, OWN_LANES:LANES] = jnp.where(keep, side, 0.0).astype(BF16)


def clear_edges(first, count, pad, row_pos):
    @pl.when(row_pos == 0)
    def _():
        pad[first : first + count, 0:HALO, :] = jnp.zeros((count, HALO, LANES), BF16)

    @pl.when(row_pos == TILE_GRID - 1)
    def _():
        pad[first : first + count, ROWS - HALO : ROWS, :] = jnp.zeros((count, HALO, LANES), BF16)


def pixel_forward(dr, dc, pad, from_left, from_right):
    src_rows = {-1: pl.ds(HALO, HALO), 0: pl.ds(HALO, 256), 1: pl.ds(256, HALO)}[dr]
    dst_rows = {-1: pl.ds(HALO + 256, HALO), 0: pl.ds(HALO, 256), 1: pl.ds(0, HALO)}[dr]
    if dc == 0:
        return pad.at[2, src_rows, pl.ds(0, OWN_LANES)], pad.at[2, dst_rows, pl.ds(0, OWN_LANES)]
    if dc < 0:
        return pad.at[2, src_rows, pl.ds(0, 128)], from_right.at[2, dst_rows, :]
    return pad.at[2, src_rows, pl.ds(OWN_LANES - 128, 128)], from_left.at[2, dst_rows, :]


def flow_kernel(sections, offsets_in, packed_in, coef, block_out,
                pad, from_left, from_right, offsets, by_row, packed, spec, kept, crossed, turned, last_row, eb, en, unit_sums, flows, cols,
                local_sem, pixel_send, pixel_recv, flow_send, flow_recv):
    tables = {name: Table(packed, name) for name in PLACES}
    sec, tile = lax.axis_index("sec"), lax.axis_index("tile")
    sec_count = lax.axis_size("sec")
    row_pos, col_pos = tile // TILE_GRID, tile % TILE_GRID

    def device(ds, dr, dc):
        row = lax.rem(row_pos + (dr + TILE_GRID), TILE_GRID)
        col = lax.rem(col_pos + (dc + TILE_GRID), TILE_GRID)
        return (lax.rem(sec + ds, sec_count), row * TILE_GRID + col)

    barrier = pltpu.get_barrier_semaphore()
    partners = [(ds, dr, dc) for ds in range(4) for dr, dc in AROUND + [(0, 0)] if (ds, dr, dc) != (0, 0, 0)]
    for p in partners:
        pl.semaphore_signal(barrier, inc=1, device_id=device(*p), device_id_type=MESH)
    own_copy = pltpu.make_async_copy(
        sections.at[:, 0], pad.at[pl.ds(0, 2), pl.ds(HALO, 256), pl.ds(0, OWN_LANES)], local_sem.at[0]
    )
    offset_copies = [
        pltpu.make_async_copy(
            offsets_in.at[c, s, 0, :, pl.ds(128 * t, 128)],
            offsets.at[c, pl.ds((4 * s + t) * 256, 256), :],
            local_sem.at[2 + 8 * c + 4 * s + t],
        )
        for c in range(2) for s in range(2) for t in range(4)
    ]
    table_copy = pltpu.make_async_copy(packed_in, packed, local_sem.at[1])
    own_copy.start()
    table_copy.start()
    for copy in offset_copies:
        copy.start()
    pl.semaphore_wait(barrier, len(partners))

    def pixel_copy(k, ds, dr, dc, refs):
        return pltpu.make_async_remote_copy(
            src_ref=refs[0], dst_ref=refs[1], send_sem=pixel_send.at[k], recv_sem=pixel_recv.at[k],
            device_id=device(ds, dr, dc), device_id_type=MESH,
        )

    both = pl.ds(0, 2)
    own = [
        pixel_copy(k, 0, dr, dc, pixel_part(dr, dc, sections, pad, from_left, from_right, both, both))
        for k, (dr, dc) in enumerate(AROUND)
    ]
    after = pixel_copy(
        8, 3, 0, 0, pixel_part(0, 0, sections, pad, from_left, from_right, pl.ds(0, 1), pl.ds(2, 1))
    )
    for copy in own + [after]:
        copy.start()

    def transform(s, group, columns):
        first_transform(s, group, columns, pad, spec, tables)

    def energies(s, blocks, lanes, columns):
        block_energies(s, blocks, lanes, pad, eb)
        node_energies(s, columns, eb, en, tables["energy_cols"])

    def units(pair, first, count):
        @pl.loop(0, count)
        def _(k):
            n = first + k
            rows_back(n - 2, turned, last_row, en, unit_sums, tables)
            columns_back(crossed, turned, last_row, tables)
            cross_unit(pair, n, spec, kept, crossed, tables)

    inner_blocks, outer_blocks = range(2, 9), (0, 1, 9, 10)
    own_lanes, side_lanes, all_lanes = slice(0, OWN_LANES), slice(OWN_LANES, LANES), slice(0, LANES)

    def inner_own(s):
        transform(s, INNER, OWN_COLS)
        energies(s, inner_blocks, own_lanes, (1, 2))

    def inner_sides(s):
        merge_sides(s, slice(HALO, HALO + 256), pad, from_left, from_right, col_pos)
        transform(s, INNER, SIDE_COLS)
        energies(s, inner_blocks, side_lanes, (0, 3))

    def outer(s):
        merge_sides(s, slice(0, HALO), pad, from_left, from_right, col_pos)
        merge_sides(s, slice(HALO + 256, ROWS), pad, from_left, from_right, col_pos)
        clear_edges(s, 1, pad, row_pos)
        transform(s, OUTER, OWN_COLS + SIDE_COLS)
        energies(s, outer_blocks, all_lanes, (0, 1, 2, 3))

    eb[...] = jnp.zeros(eb.shape, F32)
    own_copy.wait()
    table_copy.wait()
    inner_own(0)
    inner_own(1)
    cross_unit(0, 0, spec, kept, crossed, tables)
    columns_back(crossed, turned, last_row, tables)
    cross_unit(0, 1, spec, kept, crossed, tables)
    own[0].wait_recv()
    own[1].wait_recv()
    inner_sides(0)
    inner_sides(1)
    units(0, 2, 2)
    for copy in own[2:]:
        copy.wait_recv()
    outer(0)
    outer(1)
    units(0, 4, 2)
    after.wait_recv()
    forward = [
        pixel_copy(9 + k, 0, dr, dc, pixel_forward(dr, dc, pad, from_left, from_right))
        for k, (dr, dc) in enumerate(AROUND)
    ]
    for copy in forward:
        copy.start()
    units(0, 6, 2)
    inner_own(2)
    units(1, 8, 2)
    forward[0].wait_recv()
    forward[1].wait_recv()
    inner_sides(2)
    units(1, 10, 2)
    for copy in forward[2:]:
        copy.wait_recv()
    outer(2)
    units(1, 12, 4)
    rows_back(14, turned, last_row, en, unit_sums, tables)
    columns_back(crossed, turned, last_row, tables)
    rows_back(15, turned, last_row, en, unit_sums, tables)

    flows[4, sec] = flow_block(unit_sums, tables["sums"], sec == sec_count - 1)
    spread = [(ds, dr, dc) for ds in range(4) for dr, dc in AROUND + [(0, 0)] if (ds, dr, dc) != (0, 0, 0)]
    share = [
        pltpu.make_async_remote_copy(
            src_ref=flows.at[4, sec], dst_ref=flows.at[3 * (1 - dr) + 1 - dc, sec], send_sem=flow_send.at[k],
            recv_sem=flow_recv.at[k], device_id=device(ds, dr, dc), device_id_type=MESH,
        )
        for k, (ds, dr, dc) in enumerate(spread)
    ]
    for copy in share:
        copy.start()
    shifted_columns(pad, cols)
    for copy in offset_copies:
        copy.wait()

    @pl.loop(0, 32)
    def _(r):
        corners(r, offsets, by_row, cols, coef)

    for copy in share:
        copy.wait_recv()

    def column(d, c):
        return jnp.concatenate([flows[c, d], flows[3 + c, d], flows[6 + c, d]], axis=0)

    mesh = relax([extend(column(d, 1), column(d, 0), column(d, 2)) for d in range(4)], row_pos, col_pos)
    mine = mesh[0][8:16]
    for d in range(1, 4):
        mine = jnp.where(sec == d, mesh[d][8:16], mine)
    block_out[...] = mine
    for copy in own + [after] + forward + share:
        copy.wait_send()


def blend_kernel(coef, block, mesh_out, warped, by_row, result, sem):
    mesh = block[...]
    write_mesh(mesh, mesh_out)
    copies = []
    for i in range(8):
        a, b = spread_lanes(mesh, i, 0), spread_lanes(mesh, i, 1)
        for k in range(32):
            r = 32 * i + k
            first = coef[0, r] + a * coef[1, r]
            second = coef[2, r] + a * coef[3, r]
            by_row[i % 2, 8 * k : 8 * k + 8, :] = first + b * second
        for k in range(4):
            for st in range(8):
                rows = slice(256 * st + 32 * i + 8 * k, 256 * st + 32 * i + 8 * k + 8)
                result[rows, :] = by_row[i % 2, pl.ds(64 * k + st, 8, stride=8), :]
        if i % 2 == 1:
            rows = pl.ds(32 * i - 32, 64)
            for s in range(2):
                for t in range(4):
                    copy = pltpu.make_async_copy(
                        result.at[pl.ds(256 * (4 * s + t) + 32 * i - 32, 64), :],
                        warped.at[s, 0, rows, pl.ds(128 * t, 128)],
                        sem.at[len(copies)],
                    )
                    copy.start()
                    copies.append(copy)
    for copy in copies:
        copy.wait()


def vmem():
    return pl.BlockSpec(memory_space=pltpu.VMEM)


def shards(sections, corner_offsets):
    anywhere = pl.BlockSpec(memory_space=pl.ANY)
    dma = pltpu.SemaphoreType.DMA
    coef, block = pl.pallas_call(
        flow_kernel,
        out_shape=(pltpu.VMEM((4, 256, 8, 128), F32), pltpu.VMEM((8, 128), F32)),
        in_specs=[anywhere, anywhere, anywhere],
        out_specs=(vmem(), vmem()),
        scratch_shapes=[
            pltpu.VMEM((3, ROWS, LANES), BF16),
            pltpu.VMEM((3, ROWS, 128), BF16),
            pltpu.VMEM((3, ROWS, 128), BF16),
            pltpu.VMEM((2, 8 * 256, 128), jnp.int32),
            pltpu.VMEM((2, 64, 128), jnp.int32),
            pltpu.VMEM(PACKED.shape, BF16),
            pltpu.VMEM((3, 2, 5, 2, 272, 128), BF16),
            pltpu.VMEM((2, 4, 4, 272, 256), BF16),
            pltpu.VMEM((272, 1024), BF16),
            pltpu.VMEM((512, 128), BF16),
            pltpu.VMEM((8, 128), F32),
            pltpu.VMEM((3, 16, LANES), F32),
            pltpu.VMEM((3, 2, 4, 8, 128), F32),
            pltpu.VMEM((16, 8, 256), F32),
            pltpu.VMEM((9, 4, 8, 128), F32),
            pltpu.VMEM((5, 8 * SHIFT_ROWS, 128), F32),
            dma((18,)),
            dma((17,)),
            dma((17,)),
            dma((35,)),
            dma((35,)),
        ],
        compiler_params=pltpu.CompilerParams(
            vmem_limit_bytes=58 * 2**20, collective_id=0, has_side_effects=True
        ),
    )(sections, corner_offsets, jnp.asarray(PACKED))
    return pl.pallas_call(
        blend_kernel,
        out_shape=(
            jax.ShapeDtypeStruct((2, 2, 1, 8, 16), F32),
            jax.ShapeDtypeStruct((2, 1, 256, 512), F32),
        ),
        in_specs=[vmem(), vmem()],
        out_specs=(vmem(), anywhere),
        scratch_shapes=[pltpu.VMEM((2, 256, 128), F32), pltpu.VMEM((8 * 256, 128), F32), dma((32,))],
        compiler_params=pltpu.CompilerParams(vmem_limit_bytes=20 * 2**20),
    )(coef, block)


def solution(mesh):
    in_specs = (P("sec", "tile", None, None), P(None, "sec", "tile", None, None))
    out_specs = (P("sec", None, "tile", None, None), P("sec", "tile", None, None))
    return jax.shard_map(shards, mesh=mesh, in_specs=in_specs, out_specs=out_specs, check_vma=False)
```

time: 56.7 us -> 37.5 us (0.66)
  Pallas kernels: 52.3 us -> 36.8 us
  local copies, waits for them, and re-layouts: 3.59 us -> 0 us
    pallas_call x1 -> x2, Pallas kernels: 52.3 us -> 36.8 us  [the longest x1 34.7 us: shards(): pl.pallas_call(flow_kernel, out_shape=(pltpu.VMEM((4, 256, 8, 128), F32),...]
    unnamed x2 -> x0, local copies, waits for them, and re-layouts: 3.59 us -> none
where the time goes in v2:
time: 37.5 us; the launch traced here: 37.4 us
  Pallas kernels  36.8 us (98%)
  between operations  0.64 us (2%)
    pallas_call x1, Pallas kernels, shards(): pl.pallas_call(flow_kernel, out_shape=(pltpu.VMEM((4, 256, 8, 128), F32),...  34.7 us
    pallas_call x1, Pallas kernels, shards(): pl.pallas_call(blend_kernel, out_shape=(jax.ShapeDtypeStruct((2, 2, 1, 8,...  2.12 us

profile of v2, /device:TPU:1, one launch (start us, length us, event | category | flops | bytes accessed | tf_op | source)
XLA Modules:
  0.0 37.4 jit_solution(5283358939309807808)
XLA Ops:
  0.6 34.7 %shard_map.50 = (f32[4,256,8,128]{3,2,1,0:T(8,128)S(1)}, f32[8,128]{1,0:T(8,128)S(1)}) custom-call(bf16[2,1,256,512]{3,2,1,0:T(8,128)(2,1)} %sections.1, s32[2,2,1,256,512]{4,3,2,1,0:T(8,128)} %offsets_in.1, bf16[6624,128]{1,0:T(8,128)(2,1)} %constant.2.clone.packed_in), custom_call_target="tpu_custom_call" | custom-call | tf_op jit(solution)/shard_map/pallas_call | solution.py:594
  35.3 2.1 %shard_map.51 = (f32[2,2,1,8,16]{4,3,2,1,0:T(8,128)}, f32[2,1,256,512]{3,2,1,0:T(8,128)}) custom-call(f32[4,256,8,128]{3,2,1,0:T(8,128)S(1)} %get-tuple-element.4.coef, f32[8,128]{1,0:T(8,128)S(1)} %get-tuple-element.5.block), custom_call_target="tpu_custom_call" | custom-call | tf_op jit(solution)/shard_map/pallas_call | solution.py:626

commit v3 on v2

--- a/solution.py
+++ b/solution.py
@@ -313,17 +313,14 @@
     return jnp.where(odd, near[1], near[0]), jnp.where(odd, near[2], near[1])
 
 
-def corners(r, offsets, by_row, cols, coef):
+def corners(r, offsets, cols, coef):
     base = pl.multiple_of(8 * r, 8)
-    for c in range(2):
-        for st in range(8):
-            by_row[c, pl.ds(st, 8, stride=8), :] = offsets[c, pl.ds(pl.multiple_of(256 * st + base, 8), 8), :]
-    view = [
-        [cols[d, pl.ds(pl.multiple_of(8 * base + 8 * (14 + k), 8), 8), :] for d in range(5)] for k in range(12)
-    ]
+    view = []
+    for k in range(12):
+        rows = pl.ds(pl.multiple_of(8 * (base + 14 + k), 8), 8)
+        view.append([cols[d, rows, :] for d in range(5)])
     for k in range(8):
-        ro = by_row[0, 8 * k : 8 * k + 8, :]
-        co = by_row[1, 8 * k : 8 * k + 8, :]
+        ro, co = offsets[0, base + k], offsets[1, base + k]
         row_high, row_odd = ro >= 0, (ro & 1) == 1
         col_high, col_odd = co >= 0, (co & 1) == 1
         pairs = [pick_pair(col_high, col_odd, view[k + dr]) for dr in range(5)]
@@ -374,14 +371,14 @@
     pad[s, rows, OWN_LANES:LANES] = jnp.where(keep, side, 0.0).astype(BF16)
 
 
-def clear_edges(first, count, pad, row_pos):
+def clear_edges(s, pad, row_pos):
     @pl.when(row_pos == 0)
     def _():
-        pad[first : first + count, 0:HALO, :] = jnp.zeros((count, HALO, LANES), BF16)
+        pad[s, 0:HALO, :] = jnp.zeros((HALO, LANES), BF16)
 
     @pl.when(row_pos == TILE_GRID - 1)
     def _():
-        pad[first : first + count, ROWS - HALO : ROWS, :] = jnp.zeros((count, HALO, LANES), BF16)
+        pad[s, ROWS - HALO : ROWS, :] = jnp.zeros((HALO, LANES), BF16)
 
 
 def pixel_forward(dr, dc, pad, from_left, from_right):
@@ -395,7 +392,7 @@
 
 
 def flow_kernel(sections, offsets_in, packed_in, coef, block_out,
-                pad, from_left, from_right, offsets, by_row, packed, spec, kept, crossed, turned, last_row, eb, en, unit_sums, flows, cols,
+                pad, from_left, from_right, offsets, packed, spec, kept, crossed, turned, last_row, eb, en, unit_sums, flows, cols,
                 local_sem, pixel_send, pixel_recv, flow_send, flow_recv):
     tables = {name: Table(packed, name) for name in PLACES}
     sec, tile = lax.axis_index("sec"), lax.axis_index("tile")
@@ -417,7 +414,7 @@
     offset_copies = [
         pltpu.make_async_copy(
             offsets_in.at[c, s, 0, :, pl.ds(128 * t, 128)],
-            offsets.at[c, pl.ds((4 * s + t) * 256, 256), :],
+            offsets.at[c, :, 4 * s + t, :],
             local_sem.at[2 + 8 * c + 4 * s + t],
         )
         for c in range(2) for s in range(2) for t in range(4)
@@ -476,27 +473,29 @@
     def outer(s):
         merge_sides(s, slice(0, HALO), pad, from_left, from_right, col_pos)
         merge_sides(s, slice(HALO + 256, ROWS), pad, from_left, from_right, col_pos)
-        clear_edges(s, 1, pad, row_pos)
+        clear_edges(s, pad, row_pos)
         transform(s, OUTER, OWN_COLS + SIDE_COLS)
         energies(s, outer_blocks, all_lanes, (0, 1, 2, 3))
+
+    def corner_rows(first, count):
+        @pl.loop(0, count)
+        def _(k):
+            corners(first + k, offsets, cols, coef)
 
     eb[...] = jnp.zeros(eb.shape, F32)
     own_copy.wait()
     table_copy.wait()
-    inner_own(0)
-    inner_own(1)
+    pl.loop(0, 2)(inner_own)
     cross_unit(0, 0, spec, kept, crossed, tables)
     columns_back(crossed, turned, last_row, tables)
     cross_unit(0, 1, spec, kept, crossed, tables)
     own[0].wait_recv()
     own[1].wait_recv()
-    inner_sides(0)
-    inner_sides(1)
+    pl.loop(0, 2)(inner_sides)
     units(0, 2, 2)
     for copy in own[2:]:
         copy.wait_recv()
-    outer(0)
-    outer(1)
+    pl.loop(0, 2)(outer)
     units(0, 4, 2)
     after.wait_recv()
     forward = [
@@ -531,14 +530,10 @@
     ]
     for copy in share:
         copy.start()
-    shifted_columns(pad, cols)
     for copy in offset_copies:
         copy.wait()
-
-    @pl.loop(0, 32)
-    def _(r):
-        corners(r, offsets, by_row, cols, coef)
-
+    shifted_columns(pad, cols)
+    corner_rows(0, 32)
     for copy in share:
         copy.wait_recv()
 
@@ -554,7 +549,7 @@
         copy.wait_send()
 
 
-def blend_kernel(coef, block, mesh_out, warped, by_row, result, sem):
+def blend_kernel(coef, block, mesh_out, warped, result, sem):
     mesh = block[...]
     write_mesh(mesh, mesh_out)
     copies = []
@@ -564,19 +559,13 @@
             r = 32 * i + k
             first = coef[0, r] + a * coef[1, r]
             second = coef[2, r] + a * coef[3, r]
-            by_row[i % 2, 8 * k : 8 * k + 8, :] = first + b * second
-        for k in range(4):
-            for st in range(8):
-                rows = slice(256 * st + 32 * i + 8 * k, 256 * st + 32 * i + 8 * k + 8)
-                result[rows, :] = by_row[i % 2, pl.ds(64 * k + st, 8, stride=8), :]
+            result[r] = first + b * second
         if i % 2 == 1:
             rows = pl.ds(32 * i - 32, 64)
             for s in range(2):
                 for t in range(4):
                     copy = pltpu.make_async_copy(
-                        result.at[pl.ds(256 * (4 * s + t) + 32 * i - 32, 64), :],
-                        warped.at[s, 0, rows, pl.ds(128 * t, 128)],
-                        sem.at[len(copies)],
+                        result.at[rows, 4 * s + t, :], warped.at[s, 0, rows, pl.ds(128 * t, 128)], sem.at[len(copies)]
                     )
                     copy.start()
                     copies.append(copy)
@@ -600,8 +589,7 @@
             pltpu.VMEM((3, ROWS, LANES), BF16),
             pltpu.VMEM((3, ROWS, 128), BF16),
             pltpu.VMEM((3, ROWS, 128), BF16),
-            pltpu.VMEM((2, 8 * 256, 128), jnp.int32),
-            pltpu.VMEM((2, 64, 128), jnp.int32),
+            pltpu.VMEM((2, 256, 8, 128), jnp.int32),
             pltpu.VMEM(PACKED.shape, BF16),
             pltpu.VMEM((3, 2, 5, 2, 272, 128), BF16),
             pltpu.VMEM((2, 4, 4, 272, 256), BF16),
@@ -631,7 +619,7 @@
         ),
         in_specs=[vmem(), vmem()],
         out_specs=(vmem(), anywhere),
-        scratch_shapes=[pltpu.VMEM((2, 256, 128), F32), pltpu.VMEM((8 * 256, 128), F32), dma((32,))],
+        scratch_shapes=[pltpu.VMEM((256, 8, 128), F32), dma((32,))],
         compiler_params=pltpu.CompilerParams(vmem_limit_bytes=20 * 2**20),
     )(coef, block)
 

time: 37.5 us -> 37.4 us (level)
  no operation moved by 1% of the time
where the time goes in v3:
time: 37.4 us; the launch traced here: 37.3 us
  Pallas kernels  36.7 us (98%)
  between operations  0.64 us (2%)
    pallas_call x1, Pallas kernels, shards(): pl.pallas_call(flow_kernel, out_shape=(pltpu.VMEM((4, 256, 8, 128), F32),...  34.7 us
    pallas_call x1, Pallas kernels, shards(): pl.pallas_call(blend_kernel, out_shape=(jax.ShapeDtypeStruct((2, 2, 1, 8,...  1.97 us

profile of v3, /device:TPU:1, one launch (start us, length us, event | category | flops | bytes accessed | tf_op | source)
XLA Modules:
  0.0 37.3 jit_solution(11873204428252952510)
XLA Ops:
  0.6 34.7 %shard_map.50 = (f32[4,256,8,128]{3,2,1,0:T(8,128)S(1)}, f32[8,128]{1,0:T(8,128)S(1)}) custom-call(bf16[2,1,256,512]{3,2,1,0:T(8,128)(2,1)} %sections.1, s32[2,2,1,256,512]{4,3,2,1,0:T(8,128)} %offsets_in.1, bf16[6624,128]{1,0:T(8,128)(2,1)} %constant.2.clone.packed_in), custom_call_target="tpu_custom_call" | custom-call | tf_op jit(solution)/shard_map/pallas_call | solution.py:583
  35.4 2.0 %shard_map.51 = (f32[2,2,1,8,16]{4,3,2,1,0:T(8,128)}, f32[2,1,256,512]{3,2,1,0:T(8,128)}) custom-call(f32[4,256,8,128]{3,2,1,0:T(8,128)S(1)} %get-tuple-element.4.coef, f32[8,128]{1,0:T(8,128)S(1)} %get-tuple-element.5.block), custom_call_target="tpu_custom_call" | custom-call | tf_op jit(solution)/shard_map/pallas_call | solution.py:614

commit v4 on v3

--- a/solution.py
+++ b/solution.py
@@ -420,10 +420,6 @@
         for c in range(2) for s in range(2) for t in range(4)
     ]
     table_copy = pltpu.make_async_copy(packed_in, packed, local_sem.at[1])
-    own_copy.start()
-    table_copy.start()
-    for copy in offset_copies:
-        copy.start()
     pl.semaphore_wait(barrier, len(partners))
 
     def pixel_copy(k, ds, dr, dc, refs):
@@ -440,8 +436,10 @@
     after = pixel_copy(
         8, 3, 0, 0, pixel_part(0, 0, sections, pad, from_left, from_right, pl.ds(0, 1), pl.ds(2, 1))
     )
-    for copy in own + [after]:
+    for copy in [after] + own:
         copy.start()
+    own_copy.start()
+    table_copy.start()
 
     def transform(s, group, columns):
         first_transform(s, group, columns, pad, spec, tables)
@@ -486,6 +484,8 @@
     own_copy.wait()
     table_copy.wait()
     pl.loop(0, 2)(inner_own)
+    for copy in offset_copies:
+        copy.start()
     cross_unit(0, 0, spec, kept, crossed, tables)
     columns_back(crossed, turned, last_row, tables)
     cross_unit(0, 1, spec, kept, crossed, tables)
@@ -521,6 +521,7 @@
 
     flows[4, sec] = flow_block(unit_sums, tables["sums"], sec == sec_count - 1)
     spread = [(ds, dr, dc) for ds in range(4) for dr, dc in AROUND + [(0, 0)] if (ds, dr, dc) != (0, 0, 0)]
+    spread.sort(key=lambda p: (2 - abs(2 - p[0]), abs(p[1]) + abs(p[2])), reverse=True)
     share = [
         pltpu.make_async_remote_copy(
             src_ref=flows.at[4, sec], dst_ref=flows.at[3 * (1 - dr) + 1 - dc, sec], send_sem=flow_send.at[k],

time: 37.4 us -> 37.6 us (level)
  no operation moved by 1% of the time
where the time goes in v4:
time: 37.6 us; the launch traced here: 37.5 us
  Pallas kernels  36.8 us (98%)
  between operations  0.64 us (2%)
    pallas_call x1, Pallas kernels, shards(): pl.pallas_call(flow_kernel, out_shape=(pltpu.VMEM((4, 256, 8, 128), F32),...  34.9 us
    pallas_call x1, Pallas kernels, shards(): pl.pallas_call(blend_kernel, out_shape=(jax.ShapeDtypeStruct((2, 2, 1, 8,...  1.97 us

profile of v4, /device:TPU:1, one launch (start us, length us, event | category | flops | bytes accessed | tf_op | source)
XLA Modules:
  0.0 37.5 jit_solution(8404917094993809898)
XLA Ops:
  0.6 34.9 %shard_map.50 = (f32[4,256,8,128]{3,2,1,0:T(8,128)S(1)}, f32[8,128]{1,0:T(8,128)S(1)}) custom-call(bf16[2,1,256,512]{3,2,1,0:T(8,128)(2,1)} %sections.1, s32[2,2,1,256,512]{4,3,2,1,0:T(8,128)} %offsets_in.1, bf16[6624,128]{1,0:T(8,128)(2,1)} %constant.2.clone.packed_in), custom_call_target="tpu_custom_call" | custom-call | tf_op jit(solution)/shard_map/pallas_call | solution.py:584
  35.5 2.0 %shard_map.51 = (f32[2,2,1,8,16]{4,3,2,1,0:T(8,128)}, f32[2,1,256,512]{3,2,1,0:T(8,128)}) custom-call(f32[4,256,8,128]{3,2,1,0:T(8,128)S(1)} %get-tuple-element.4.coef, f32[8,128]{1,0:T(8,128)S(1)} %get-tuple-element.5.block), custom_call_target="tpu_custom_call" | custom-call | tf_op jit(solution)/shard_map/pallas_call | solution.py:615

commit v5 on v3

--- a/solution.py
+++ b/solution.py
@@ -297,15 +297,13 @@
 SHIFT_ROWS = 288
 
 
-def shifted_columns(pad, cols):
-    @pl.loop(0, SHIFT_ROWS // 16)
-    def _(k):
-        for s in range(2):
-            x = pad[s, pl.ds(pl.multiple_of(32 + 16 * k, 16), 16), :].astype(F32)
-            for d in range(5):
-                y = x if d == 2 else pltpu.roll(x, (2 - d) % LANES, 1)
-                for t in range(4):
-                    cols[d, pl.ds(128 * k + (4 * s + t), 16, stride=8), :] = y[:, 128 * t : 128 * t + 128]
+def shifted_columns(k, pad, cols):
+    for s in range(2):
+        x = pad[s, pl.ds(pl.multiple_of(32 + 16 * k, 16), 16), :].astype(F32)
+        for d in range(5):
+            y = x if d == 2 else pltpu.roll(x, (2 - d) % LANES, 1)
+            for t in range(4):
+                cols[d, pl.ds(128 * k + (4 * s + t), 16, stride=8), :] = y[:, 128 * t : 128 * t + 128]
 
 
 def pick_pair(high, odd, values):
@@ -450,13 +448,21 @@
         block_energies(s, blocks, lanes, pad, eb)
         node_energies(s, columns, eb, en, tables["energy_cols"])
 
-    def units(pair, first, count):
+    def units(pair, first, count, beside=lambda k: None):
         @pl.loop(0, count)
         def _(k):
             n = first + k
             rows_back(n - 2, turned, last_row, en, unit_sums, tables)
             columns_back(crossed, turned, last_row, tables)
             cross_unit(pair, n, spec, kept, crossed, tables)
+            beside(k)
+
+    def shifts(first, each):
+        def run(k):
+            for i in range(each):
+                shifted_columns(first + each * k + i, pad, cols)
+
+        return run
 
     inner_blocks, outer_blocks = range(2, 9), (0, 1, 9, 10)
     own_lanes, side_lanes, all_lanes = slice(0, OWN_LANES), slice(OWN_LANES, LANES), slice(0, LANES)
@@ -496,7 +502,7 @@
     for copy in own[2:]:
         copy.wait_recv()
     pl.loop(0, 2)(outer)
-    units(0, 4, 2)
+    units(0, 4, 2, shifts(0, 5))
     after.wait_recv()
     forward = [
         pixel_copy(9 + k, 0, dr, dc, pixel_forward(dr, dc, pad, from_left, from_right))
@@ -504,7 +510,7 @@
     ]
     for copy in forward:
         copy.start()
-    units(0, 6, 2)
+    units(0, 6, 2, shifts(10, 4))
     inner_own(2)
     units(1, 8, 2)
     forward[0].wait_recv()
@@ -532,7 +538,6 @@
         copy.start()
     for copy in offset_copies:
         copy.wait()
-    shifted_columns(pad, cols)
     corner_rows(0, 32)
     for copy in share:
         copy.wait_recv()

time: 37.4 us -> 37.8 us (1.011)
  Pallas kernels: 36.7 us -> 37.1 us
where the time goes in v5:
time: 37.8 us; the launch traced here: 37.7 us
  Pallas kernels  37.1 us (98%)
  between operations  0.64 us (2%)
    pallas_call x1, Pallas kernels, shards(): pl.pallas_call(flow_kernel, out_shape=(pltpu.VMEM((4, 256, 8, 128), F32),...  35.1 us
    pallas_call x1, Pallas kernels, shards(): pl.pallas_call(blend_kernel, out_shape=(jax.ShapeDtypeStruct((2, 2, 1, 8,...  1.97 us

profile of v5, /device:TPU:1, one launch (start us, length us, event | category | flops | bytes accessed | tf_op | source)
XLA Modules:
  0.0 37.7 jit_solution(6508424502869555930)
XLA Ops:
  0.6 35.1 %shard_map.50 = (f32[4,256,8,128]{3,2,1,0:T(8,128)S(1)}, f32[8,128]{1,0:T(8,128)S(1)}) custom-call(bf16[2,1,256,512]{3,2,1,0:T(8,128)(2,1)} %sections.1, s32[2,2,1,256,512]{4,3,2,1,0:T(8,128)} %offsets_in.1, bf16[6624,128]{1,0:T(8,128)(2,1)} %constant.2.clone.packed_in), custom_call_target="tpu_custom_call" | custom-call | tf_op jit(solution)/shard_map/pallas_call | solution.py:588
  35.7 2.0 %shard_map.51 = (f32[2,2,1,8,16]{4,3,2,1,0:T(8,128)}, f32[2,1,256,512]{3,2,1,0:T(8,128)}) custom-call(f32[4,256,8,128]{3,2,1,0:T(8,128)S(1)} %get-tuple-element.4.coef, f32[8,128]{1,0:T(8,128)S(1)} %get-tuple-element.5.block), custom_call_target="tpu_custom_call" | custom-call | tf_op jit(solution)/shard_map/pallas_call | solution.py:619

commit v6 on v3

--- a/solution.py
+++ b/solution.py
@@ -267,29 +267,24 @@
     count = len(flow)
     zero = jnp.zeros(shape, F32)
 
-    def following(f):
-        turned = [pltpu.roll(x, 64, 1) for x in f] + [zero]
-        return [jnp.where(low, turned[d], turned[d + 1]) for d in range(count)]
-
-    def preceding(f):
-        turned = [zero] + [pltpu.roll(x, 64, 1) for x in f]
-        return [jnp.where(low, turned[d], turned[d + 1]) for d in range(count)]
+    def beside_sections(f):
+        turned = [zero] + [pltpu.roll(x, 64, 1) for x in f] + [zero]
+        later = [jnp.where(low, turned[d + 1], turned[d + 2]) for d in range(count)]
+        earlier = [jnp.where(low, turned[d], turned[d + 1]) for d in range(count)]
+        return later, earlier
 
     flow = [f * mask for f in flow]
-    mesh = [zero] * count
-    for step in range(ITERS):
-        if step == 0:
-            spring = [-f for f in flow]
-        else:
-            spring = [m - n - f for m, n, f in zip(mesh, following(mesh), flow)]
-        earlier = preceding(spring)
+    before = beside_sections(flow)[1]
+    pull = [(STEP_RATE * mask) * (f - p) for f, p in zip(flow, before)]
+    mesh = pull
+    rate = STEP_RATE * mask
+    for step in range(1, ITERS):
+        later, earlier = beside_sections(mesh)
         updated = []
-        for m, sp, ea in zip(mesh, spring, earlier):
-            change = sp - ea
-            if step > 0:
-                around = pltpu.roll(m, 1, 0) + pltpu.roll(m, 23, 0) + pltpu.roll(m, 1, 1) + pltpu.roll(m, 127, 1)
-                change = change + 4.0 * m - around
-            updated.append((m - STEP_RATE * change) * mask)
+        for d, m in enumerate(mesh):
+            own = 6.0 if d > 0 else jnp.where(low, 5.0, 6.0)
+            around = pltpu.roll(m, 1, 0) + pltpu.roll(m, 23, 0) + pltpu.roll(m, 1, 1) + pltpu.roll(m, 127, 1)
+            updated.append(m - rate * (own * m - later[d] - earlier[d] - around) + pull[d])
         mesh = updated
     return mesh
 
@@ -405,7 +400,10 @@
         return (lax.rem(sec + ds, sec_count), row * TILE_GRID + col)
 
     barrier = pltpu.get_barrier_semaphore()
-    partners = [(ds, dr, dc) for ds in range(4) for dr, dc in AROUND + [(0, 0)] if (ds, dr, dc) != (0, 0, 0)]
+    partners = [
+        (ds, dr, dc) for ds in range(4) for dr, dc in AROUND + [(0, 0)]
+        if (ds, dr, dc) != (0, 0, 0) and not (ds == 2 and dr * dc != 0)
+    ]
     for p in partners:
         pl.semaphore_signal(barrier, inc=1, device_id=device(*p), device_id_type=MESH)
     own_copy = pltpu.make_async_copy(
@@ -483,6 +481,8 @@
             corners(first + k, offsets, cols, coef)
 
     eb[...] = jnp.zeros(eb.shape, F32)
+    for slot in (0, 2, 6, 8):
+        flows[slot, lax.rem(sec + 2, sec_count)] = jnp.zeros((8, 128), F32)
     own_copy.wait()
     table_copy.wait()
     pl.loop(0, 2)(inner_own)
@@ -520,13 +520,12 @@
     rows_back(15, turned, last_row, en, unit_sums, tables)
 
     flows[4, sec] = flow_block(unit_sums, tables["sums"], sec == sec_count - 1)
-    spread = [(ds, dr, dc) for ds in range(4) for dr, dc in AROUND + [(0, 0)] if (ds, dr, dc) != (0, 0, 0)]
     share = [
         pltpu.make_async_remote_copy(
             src_ref=flows.at[4, sec], dst_ref=flows.at[3 * (1 - dr) + 1 - dc, sec], send_sem=flow_send.at[k],
             recv_sem=flow_recv.at[k], device_id=device(ds, dr, dc), device_id_type=MESH,
         )
-        for k, (ds, dr, dc) in enumerate(spread)
+        for k, (ds, dr, dc) in enumerate(partners)
     ]
     for copy in share:
         copy.start()
@@ -534,6 +533,8 @@
         copy.wait()
     shifted_columns(pad, cols)
     corner_rows(0, 32)
+    for copy in own + [after] + forward + share:
+        copy.wait_send()
     for copy in share:
         copy.wait_recv()
 
@@ -545,8 +546,6 @@
     for d in range(1, 4):
         mine = jnp.where(sec == d, mesh[d][8:16], mine)
     block_out[...] = mine
-    for copy in own + [after] + forward + share:
-        copy.wait_send()
 
 
 def blend_kernel(coef, block, mesh_out, warped, result, sem):
@@ -604,8 +603,8 @@
             dma((18,)),
             dma((17,)),
             dma((17,)),
-            dma((35,)),
-            dma((35,)),
+            dma((31,)),
+            dma((31,)),
         ],
         compiler_params=pltpu.CompilerParams(
             vmem_limit_bytes=58 * 2**20, collective_id=0, has_side_effects=True

time: 37.4 us -> 36.1 us (0.965)
  Pallas kernels: 36.7 us -> 35.4 us
    pallas_call x1, Pallas kernels: 34.7 us -> 33.4 us  [shards(): pl.pallas_call(flow_kernel, out_shape=(pltpu.VMEM((4, 256, 8, 128), F32),...]
where the time goes in v6:
time: 36.1 us; the launch traced here: 36 us
  Pallas kernels  35.4 us (98%)
  between operations  0.64 us (2%)
    pallas_call x1, Pallas kernels, shards(): pl.pallas_call(flow_kernel, out_shape=(pltpu.VMEM((4, 256, 8, 128), F32),...  33.4 us
    pallas_call x1, Pallas kernels, shards(): pl.pallas_call(blend_kernel, out_shape=(jax.ShapeDtypeStruct((2, 2, 1, 8,...  1.97 us

profile of v6, /device:TPU:1, one launch (start us, length us, event | category | flops | bytes accessed | tf_op | source)
XLA Modules:
  0.0 36.0 jit_solution(15158833168033475344)
XLA Ops:
  0.6 33.4 %shard_map.50 = (f32[4,256,8,128]{3,2,1,0:T(8,128)S(1)}, f32[8,128]{1,0:T(8,128)S(1)}) custom-call(bf16[2,1,256,512]{3,2,1,0:T(8,128)(2,1)} %sections.1, s32[2,2,1,256,512]{4,3,2,1,0:T(8,128)} %offsets_in.1, bf16[6624,128]{1,0:T(8,128)(2,1)} %constant.2.clone.packed_in), custom_call_target="tpu_custom_call" | custom-call | tf_op jit(solution)/shard_map/pallas_call | solution.py:582
  34.0 2.0 %shard_map.51 = (f32[2,2,1,8,16]{4,3,2,1,0:T(8,128)}, f32[2,1,256,512]{3,2,1,0:T(8,128)}) custom-call(f32[4,256,8,128]{3,2,1,0:T(8,128)S(1)} %get-tuple-element.4.coef, f32[8,128]{1,0:T(8,128)S(1)} %get-tuple-element.5.block), custom_call_target="tpu_custom_call" | custom-call | tf_op jit(solution)/shard_map/pallas_call | solution.py:613

commit v7 on v6

--- a/solution.py
+++ b/solution.py
@@ -1,3 +1,4 @@
+import functools
 import math
 
 import jax
@@ -404,8 +405,41 @@
         (ds, dr, dc) for ds in range(4) for dr, dc in AROUND + [(0, 0)]
         if (ds, dr, dc) != (0, 0, 0) and not (ds == 2 and dr * dc != 0)
     ]
-    for p in partners:
-        pl.semaphore_signal(barrier, inc=1, device_id=device(*p), device_id_type=MESH)
+    flows[...] = jnp.zeros(flows.shape, F32)
+
+    def there(dr, dc):
+        row, col = row_pos + dr, col_pos + dc
+        return (row >= 0) & (row < TILE_GRID) & (col >= 0) & (col < TILE_GRID)
+
+    def toward(dr, dc, action):
+        if (dr, dc) == (0, 0):
+            action()
+        else:
+            pl.when(there(dr, dc))(action)
+
+    def start_all(copies):
+        for way in AROUND + [(0, 0)]:
+            toward(*way, lambda way=way: [c.start() for w, c in copies if w == way] and None)
+
+    def wait_sent(copies):
+        for way in AROUND + [(0, 0)]:
+            toward(*way, lambda way=way: [c.wait_send() for w, c in copies if w == way] and None)
+
+    def wait_come(copies):
+        for way in AROUND + [(0, 0)]:
+            if any(w == way for w, _ in copies):
+                toward(-way[0], -way[1], lambda way=way: [c.wait_recv() for w, c in copies if w == way] and None)
+
+    def greet(way):
+        for p in partners:
+            if p[1:] == way:
+                pl.semaphore_signal(barrier, inc=1, device_id=device(*p), device_id_type=MESH)
+
+    expected = jnp.int32(0)
+    for way in AROUND + [(0, 0)]:
+        toward(*way, functools.partial(greet, way))
+        count = sum(p[1:] == way for p in partners)
+        expected += count if way == (0, 0) else count * there(*way).astype(jnp.int32)
     own_copy = pltpu.make_async_copy(
         sections.at[:, 0], pad.at[pl.ds(0, 2), pl.ds(HALO, 256), pl.ds(0, OWN_LANES)], local_sem.at[0]
     )
@@ -422,7 +456,7 @@
     table_copy.start()
     for copy in offset_copies:
         copy.start()
-    pl.semaphore_wait(barrier, len(partners))
+    pl.semaphore_wait(barrier, expected)
 
     def pixel_copy(k, ds, dr, dc, refs):
         return pltpu.make_async_remote_copy(
@@ -432,14 +466,14 @@
 
     both = pl.ds(0, 2)
     own = [
-        pixel_copy(k, 0, dr, dc, pixel_part(dr, dc, sections, pad, from_left, from_right, both, both))
+        ((dr, dc), pixel_copy(k, 0, dr, dc, pixel_part(dr, dc, sections, pad, from_left, from_right, both, both)))
         for k, (dr, dc) in enumerate(AROUND)
     ]
     after = pixel_copy(
         8, 3, 0, 0, pixel_part(0, 0, sections, pad, from_left, from_right, pl.ds(0, 1), pl.ds(2, 1))
     )
-    for copy in own + [after]:
-        copy.start()
+    start_all(own)
+    after.start()
 
     def transform(s, group, columns):
         first_transform(s, group, columns, pad, spec, tables)
@@ -481,38 +515,31 @@
             corners(first + k, offsets, cols, coef)
 
     eb[...] = jnp.zeros(eb.shape, F32)
-    for slot in (0, 2, 6, 8):
-        flows[slot, lax.rem(sec + 2, sec_count)] = jnp.zeros((8, 128), F32)
     own_copy.wait()
     table_copy.wait()
     pl.loop(0, 2)(inner_own)
     cross_unit(0, 0, spec, kept, crossed, tables)
     columns_back(crossed, turned, last_row, tables)
     cross_unit(0, 1, spec, kept, crossed, tables)
-    own[0].wait_recv()
-    own[1].wait_recv()
+    wait_come(own[:2])
     pl.loop(0, 2)(inner_sides)
     units(0, 2, 2)
-    for copy in own[2:]:
-        copy.wait_recv()
+    wait_come(own[2:])
     pl.loop(0, 2)(outer)
     units(0, 4, 2)
     after.wait_recv()
     forward = [
-        pixel_copy(9 + k, 0, dr, dc, pixel_forward(dr, dc, pad, from_left, from_right))
+        ((dr, dc), pixel_copy(9 + k, 0, dr, dc, pixel_forward(dr, dc, pad, from_left, from_right)))
         for k, (dr, dc) in enumerate(AROUND)
     ]
-    for copy in forward:
-        copy.start()
+    start_all(forward)
     units(0, 6, 2)
     inner_own(2)
     units(1, 8, 2)
-    forward[0].wait_recv()
-    forward[1].wait_recv()
+    wait_come(forward[:2])
     inner_sides(2)
     units(1, 10, 2)
-    for copy in forward[2:]:
-        copy.wait_recv()
+    wait_come(forward[2:])
     outer(2)
     units(1, 12, 4)
     rows_back(14, turned, last_row, en, unit_sums, tables)
@@ -521,22 +548,20 @@
 
     flows[4, sec] = flow_block(unit_sums, tables["sums"], sec == sec_count - 1)
     share = [
-        pltpu.make_async_remote_copy(
+        ((dr, dc), pltpu.make_async_remote_copy(
             src_ref=flows.at[4, sec], dst_ref=flows.at[3 * (1 - dr) + 1 - dc, sec], send_sem=flow_send.at[k],
             recv_sem=flow_recv.at[k], device_id=device(ds, dr, dc), device_id_type=MESH,
-        )
+        ))
         for k, (ds, dr, dc) in enumerate(partners)
     ]
-    for copy in share:
-        copy.start()
+    start_all(share)
     for copy in offset_copies:
         copy.wait()
     shifted_columns(pad, cols)
     corner_rows(0, 32)
-    for copy in own + [after] + forward + share:
-        copy.wait_send()
-    for copy in share:
-        copy.wait_recv()
+    wait_sent(own + forward + share)
+    after.wait_send()
+    wait_come(share)
 
     def column(d, c):
         return jnp.concatenate([flows[c, d], flows[3 + c, d], flows[6 + c, d]], axis=0)

time: 36.1 us -> 33.1 us (0.917)
  Pallas kernels: 35.4 us -> 32.4 us
    pallas_call x1, Pallas kernels: 33.4 us -> 30.4 us  [shards(): pl.pallas_call(flow_kernel, out_shape=(pltpu.VMEM((4, 256, 8, 128), F32),...]
where the time goes in v7:
time: 33.1 us; the launch traced here: 33 us
  Pallas kernels  32.4 us (98%)
  between operations  0.64 us (2%)
    pallas_call x1, Pallas kernels, shards(): pl.pallas_call(flow_kernel, out_shape=(pltpu.VMEM((4, 256, 8, 128), F32),...  30.4 us
    pallas_call x1, Pallas kernels, shards(): pl.pallas_call(blend_kernel, out_shape=(jax.ShapeDtypeStruct((2, 2, 1, 8,...  1.97 us

profile of v7, /device:TPU:1, one launch (start us, length us, event | category | flops | bytes accessed | tf_op | source)
XLA Modules:
  0.0 33.0 jit_solution(6280881245843066537)
XLA Ops:
  0.6 30.4 %shard_map.50 = (f32[4,256,8,128]{3,2,1,0:T(8,128)S(1)}, f32[8,128]{1,0:T(8,128)S(1)}) custom-call(bf16[2,1,256,512]{3,2,1,0:T(8,128)(2,1)} %sections.1, s32[2,2,1,256,512]{4,3,2,1,0:T(8,128)} %offsets_in.1, bf16[6624,128]{1,0:T(8,128)(2,1)} %constant.2.clone.packed_in), custom_call_target="tpu_custom_call" | custom-call | tf_op jit(solution)/shard_map/pallas_call | solution.py:607
  31.0 2.0 %shard_map.51 = (f32[2,2,1,8,16]{4,3,2,1,0:T(8,128)}, f32[2,1,256,512]{3,2,1,0:T(8,128)}) custom-call(f32[4,256,8,128]{3,2,1,0:T(8,128)S(1)} %get-tuple-element.4.coef, f32[8,128]{1,0:T(8,128)S(1)} %get-tuple-element.5.block), custom_call_target="tpu_custom_call" | custom-call | tf_op jit(solution)/shard_map/pallas_call | solution.py:638
